TPU v7x, 256 devices: a whole 4x4x8 slice. The times are simulated.
256 devices in a mesh: dp: 32 (over x, y, core), fsdp: 8 (over z).
Axes of the slice: x: 4, y: 4, z: 8, core: 2. Of those that a mesh axis runs over, the one named last changes fastest.
Arguments:
- patches: bfloat16 [131072, 1280], P(('dp', 'fsdp')), may hold values from -24 to 24
- patch_count: int32 [8192], P(('dp', 'fsdp')), may hold values from 1 to 16, as said below
- destination: int32 [8192], P(('dp', 'fsdp')), may hold values from 0 to 31, as said below
- qkv_weight: bfloat16 [1280, 1920], P('fsdp'), may hold values from -0.15625 to 0.15625
- qkv_bias: bfloat16 [1920], P('fsdp'), may hold values from -8 to 8
- norm_gain: bfloat16 [1280], P('fsdp'), may hold values from 0.099609375 to 1.8984375
- grad_out: bfloat16 [229376, 640], P(('dp', 'fsdp')), may hold values from -6 to 6
Outputs:
- attended: bfloat16 [229376, 640], P(('dp', 'fsdp'))
- grad_patches: bfloat16 [131072, 1280], P(('dp', 'fsdp'))
- grad_weight: float32 [1280, 1920], P('fsdp')
- grad_bias: float32 [1920], P('fsdp')
- grad_gain: float32 [1280], P('fsdp')
Inputs may be any that keep to these rules, and one draw needn't show every extreme that they name: `destination`: the receiver of image i sits at the same index along fsdp as the device that holds it. Among one device's images at most 2 name the same receiver, and some device sends exactly 2 to one receiver; every device receives at most 56 images, and some device receives exactly 56. `patch_count`: every device holds an image with 16 real patches.
All inputs are finite; a program needn't handle non-finite values.
Results may differ from a plain program's by a relative error of at most 0.018.
The roundings to bfloat16 on the way count: a program that leaves them out, or rounds other values in their place, can miss the bound.
Values may be sent and summed in bfloat16 or wider, within the bound.
A program may use at most 128 MiB of HBM per device.

v0:
```python
import math

import jax
import jax.numpy as jnp
from jax import lax
from jax.sharding import PartitionSpec as P

HEADS = 8
HEAD_DIM = 80


def forward(block_images, counts, weight, bias_full, gain_full):
    batch, rows, model_width = block_images.shape
    rows_f32 = block_images.astype(jnp.float32)
    inverse_rms = lax.rsqrt(jnp.mean(rows_f32 * rows_f32, axis=-1, keepdims=True) + 1e-06)
    normed = (rows_f32 * inverse_rms * gain_full.astype(jnp.float32)).astype(jnp.bfloat16)
    normed_flat = normed.reshape(batch * rows, model_width)
    projected = jnp.dot(normed_flat, weight, preferred_element_type=jnp.float32) + bias_full.astype(
        jnp.float32
    )
    packed = projected.astype(jnp.bfloat16).reshape(batch, rows, 3, HEADS, HEAD_DIM)
    query = packed[:, :, 0]
    keyset = packed[:, :, 1]
    values = packed[:, :, 2]
    score_scale = 1.0 / math.sqrt(HEAD_DIM)
    scores = (
        jnp.einsum("bqhe,bkhe->bhqk", query, keyset, preferred_element_type=jnp.float32)
        * score_scale
    )
    slot_index = jnp.arange(rows, dtype=jnp.int32)
    key_valid = slot_index[None, :] < jnp.maximum(counts, 1)[:, None]
    scores = jnp.where(key_valid[:, None, None, :], scores, -1e30)
    row_top = jnp.max(scores, axis=-1, keepdims=True)
    exponent = jnp.exp(scores - row_top)
    attention = exponent / jnp.sum(exponent, axis=-1, keepdims=True)
    attention_b = attention.astype(jnp.bfloat16)
    context = jnp.einsum("bhqk,bkhe->bqhe", attention_b, values, preferred_element_type=jnp.float32)
    row_valid = slot_index[None, :] < counts[:, None]
    output = (
        context.reshape(batch, rows, HEADS * HEAD_DIM) * row_valid[:, :, None].astype(jnp.float32)
    ).astype(jnp.bfloat16)
    kept_state = (
        rows_f32,
        inverse_rms,
        normed_flat,
        query,
        keyset,
        values,
        attention,
        attention_b,
        row_valid,
    )
    return (output, kept_state)


def backward(kept_state, cotangent, weight, gain_full):
    rows_f32, inverse_rms, normed_flat, query, keyset, values, attention, attention_b, row_valid = (
        kept_state
    )
    batch, rows, model_width = rows_f32.shape
    score_scale = 1.0 / math.sqrt(HEAD_DIM)
    grad_rows = (cotangent * row_valid[:, :, None].astype(jnp.bfloat16)).reshape(
        batch, rows, HEADS, HEAD_DIM
    )
    d_values = jnp.einsum(
        "bhqk,bqhe->bkhe", attention_b, grad_rows, preferred_element_type=jnp.float32
    )
    d_attention = jnp.einsum(
        "bqhe,bkhe->bhqk", grad_rows, values, preferred_element_type=jnp.float32
    )
    d_scores = (
        attention
        * (d_attention - jnp.sum(d_attention * attention, axis=-1, keepdims=True))
        * score_scale
    )
    d_scores_b = d_scores.astype(jnp.bfloat16)
    d_query = jnp.einsum("bhqk,bkhe->bqhe", d_scores_b, keyset, preferred_element_type=jnp.float32)
    d_keys = jnp.einsum("bhqk,bqhe->bkhe", d_scores_b, query, preferred_element_type=jnp.float32)
    d_packed = (
        jnp.stack([d_query, d_keys, d_values], axis=2)
        .astype(jnp.bfloat16)
        .reshape(batch * rows, 3 * HEADS * HEAD_DIM)
    )
    d_weight = lax.dot_general(
        normed_flat, d_packed, (((0,), (0,)), ((), ())), preferred_element_type=jnp.float32
    )
    d_bias = jnp.sum(d_packed, axis=0, dtype=jnp.float32)
    d_normed = lax.dot_general(
        d_packed, weight, (((1,), (1,)), ((), ())), preferred_element_type=jnp.float32
    ).reshape(batch, rows, model_width)
    scaled = d_normed * gain_full.astype(jnp.float32)
    d_gain = jnp.sum(d_normed * rows_f32 * inverse_rms, axis=(0, 1))
    d_images = inverse_rms * scaled - rows_f32 * inverse_rms**3 * jnp.mean(
        scaled * rows_f32, axis=-1, keepdims=True
    )
    return (d_images.astype(jnp.bfloat16), d_weight, d_bias, d_gain)


def local(patches, patch_count, destination, qkv_weight, qkv_bias, norm_gain, grad_out):
    dp_count = lax.axis_size("dp")
    fsdp_count = lax.axis_size("fsdp")
    images_here = patch_count.shape[0]
    slot_len = patches.shape[0] // images_here
    model_width = patches.shape[1]
    head_cols = grad_out.shape[1]
    received_max = grad_out.shape[0] // slot_len
    quarter = dp_count // 4
    per_peer = (13 + quarter) // quarter
    lane_count = dp_count * per_peer
    weight, bias_full, gain_full = (
        lax.all_gather(qkv_weight, "fsdp", axis=0, tiled=True),
        lax.all_gather(qkv_bias, "fsdp", axis=0, tiled=True),
        lax.all_gather(norm_gain, "fsdp", axis=0, tiled=True),
    )
    images = patches.reshape(images_here, slot_len, model_width)
    target_marks = (destination[:, None] == jnp.arange(dp_count, dtype=jnp.int32)[None, :]).astype(
        jnp.int32
    )
    earlier = jnp.cumsum(target_marks, axis=0) - target_marks
    position = jnp.sum(earlier * target_marks, axis=1)
    lane_of = destination * per_peer + position
    placing = (lane_of[:, None] == jnp.arange(lane_count, dtype=jnp.int32)[None, :]).astype(
        jnp.bfloat16
    )
    count_column = patch_count.astype(jnp.bfloat16)[:, None]

    def to_lanes(source_rows):
        flattened = source_rows.reshape(images_here, -1)
        relocated = lax.dot_general(
            placing, flattened, (((0,), (0,)), ((), ())), preferred_element_type=jnp.float32
        )
        return relocated.astype(jnp.bfloat16).reshape((dp_count, per_peer) + source_rows.shape[1:])

    slot_grads = grad_out.reshape(received_max, slot_len, head_cols)
    arrived, arrived_counts = (
        lax.all_to_all(to_lanes(images), "dp", split_axis=0, concat_axis=0, tiled=True),
        lax.all_to_all(to_lanes(count_column), "dp", split_axis=0, concat_axis=0, tiled=True),
    )
    counts_int = arrived_counts.reshape(lane_count).astype(jnp.int32)
    filled = (counts_int > 0).astype(jnp.int32)
    lane_rank = jnp.cumsum(filled) - 1
    chosen = (lane_rank[None, :] == jnp.arange(received_max, dtype=jnp.int32)[:, None]) & (
        filled[None, :] > 0
    )
    local_counts = jnp.sum(chosen.astype(jnp.int32) * counts_int[None, :], axis=1)
    picker, local_counts = (chosen.astype(jnp.bfloat16), local_counts)
    flattened = arrived.reshape(lane_count, -1)
    relocated = jnp.dot(picker, flattened, preferred_element_type=jnp.float32)
    gathered = relocated.astype(jnp.bfloat16).reshape((received_max,) + arrived.shape[2:])
    attended, kept_state = forward(gathered, local_counts, weight, bias_full, gain_full)
    grad_local, d_weight, d_bias, d_gain = backward(kept_state, slot_grads, weight, gain_full)
    flattened = grad_local.reshape(received_max, -1)
    relocated = lax.dot_general(
        picker, flattened, (((0,), (0,)), ((), ())), preferred_element_type=jnp.float32
    )
    returned_rows = lax.all_to_all(
        relocated.astype(jnp.bfloat16).reshape((dp_count, per_peer) + grad_local.shape[1:]),
        "dp",
        split_axis=0,
        concat_axis=0,
        tiled=True,
    )
    flattened = returned_rows.reshape(lane_count, -1)
    relocated = jnp.dot(placing, flattened, preferred_element_type=jnp.float32)
    grad_images = relocated.astype(jnp.bfloat16).reshape((images_here,) + returned_rows.shape[2:])
    shard_sums = (
        lax.psum_scatter(
            d_weight.astype(jnp.bfloat16), "fsdp", scatter_dimension=0, tiled=True
        ).astype(jnp.float32),
        lax.psum_scatter(
            d_bias.astype(jnp.bfloat16), "fsdp", scatter_dimension=0, tiled=True
        ).astype(jnp.float32),
        lax.psum_scatter(
            d_gain.astype(jnp.bfloat16), "fsdp", scatter_dimension=0, tiled=True
        ).astype(jnp.float32),
    )
    weight_sum, bias_sum, gain_sum = lax.psum((shard_sums[0], shard_sums[1], shard_sums[2]), "dp")
    grad_scale = 1.0 / math.sqrt(dp_count * fsdp_count * images_here * slot_len)
    return (
        attended.reshape(received_max * slot_len, head_cols),
        grad_images.reshape(images_here * slot_len, model_width),
        weight_sum * grad_scale,
        bias_sum * grad_scale,
        gain_sum * grad_scale,
    )


def solution(mesh):
    return jax.shard_map(
        local,
        mesh=mesh,
        in_specs=(
            P(("dp", "fsdp"), None),
            P(("dp", "fsdp")),
            P(("dp", "fsdp")),
            P("fsdp", None),
            P("fsdp"),
            P("fsdp"),
            P(("dp", "fsdp"), None),
        ),
        out_specs=(
            P(("dp", "fsdp"), None),
            P(("dp", "fsdp"), None),
            P("fsdp", None),
            P("fsdp"),
            P("fsdp"),
        ),
        check_vma=False,
    )
```

profile of v0, /device:TPU:32, one launch (start us, length us, event | category | flops | bytes accessed | tf_op | source)
XLA Modules:
  0.0 381.6 jit_solution(341201891159563676)
XLA Ops:
  7.2 0.7 all-gather.2.cloned.1.call-update
  7.9 0.7 fusion.31
  8.7 0.8 select_reduce_fusion.1
  9.5 0.7 multiply_add_fusion
  10.2 0.8 fusion.16
  11.0 0.7 reshape.255
  11.8 7.3 %all-to-all-start = ((bf16[32,2,1]{1,2,0:T(2,128)(2,1)}), bf16[32,2,1]{1,2,0:T(2,128)(2,1)S(1)}, u32[]{:S(2)}, u32[]{:S(2)}) async-start(bf16[32,2,1]{1,2,0:T(2,128)(2,1)} %reshape.255), calls=%async_computation | async-start | bytes 32768 | tf_op jit(solution)/shard_map/all_to_all | solution.py:137
  19.1 1.7 reshape_reshape.6
  20.8 1.0 convolution_convert_fusion.1
  21.8 2.0 copy.56
  23.8 2.6 all-to-all-done
  26.4 5.0 %all-to-all-start.1 = ((bf16[32,2,16,1280]{3,2,1,0:T(8,128)(2,1)}), bf16[32,2,16,1280]{3,2,1,0:T(8,128)(2,1)S(1)}, u32[]{:S(2)}, u32[]{:S(2)}) async-start(bf16[32,2,16,1280]{3,2,1,0:T(8,128)(2,1)} %bitcast.21), calls=%async_computation.1 | async-start | bytes 5242880 | tf_op jit(solution)/shard_map/all_to_all | solution.py:136
  31.4 0.6 fusion.48
  33.3 0.2 dynamic-update-slice
  33.6 0.2 dynamic-update-slice.1
  33.8 18.5 %all-reduce.6 = (bf16[1920]{0:T(1024)(128)(2,1)S(1)}, bf16[1280]{0:T(1024)(128)(2,1)S(1)}) all-reduce(bf16[1920]{0:T(1024)(128)(2,1)S(1)} %dynamic-update-slice.1, bf16[1280]{0:T(1024)(128)(2,1)S(1)} %dynamic-update-slice), channel_id=1, replica_groups=mesh['dp'=32,'fsdp'=8] {'fsdp'}, use_global_device_ids=true, to_apply=%add.1 | all-reduce | flops 3200 | bytes 12800
  52.3 0.6 convert_element_type.189
  53.0 4.4 %reshape.233 = bf16[56,16,8,80]{3,2,1,0:T(8,128)(2,1)} reshape(bf16[896,640]{1,0:T(8,128)(2,1)} %param.13) | data formatting | bytes 2293760 | tf_op jit(solution)/shard_map/reshape | solution.py:134
  57.9 0.7 iota_compare_fusion.1
  58.7 7.3 %all-to-all-done.1 = bf16[32,2,16,1280]{3,2,1,0:T(8,128)(2,1)S(1)} async-done(((bf16[32,2,16,1280]{3,2,1,0:T(8,128)(2,1)}), bf16[32,2,16,1280]{3,2,1,0:T(8,128)(2,1)S(1)}, u32[]{:S(2)}, u32[]{:S(2)}) %all-to-all-start.1) | async-done | bytes 2621472 | tf_op jit(solution)/shard_map/all_to_all | solution.py:136
  66.0 0.9 copy.57
  66.9 2.8 fusion.2
  69.7 5.8 %reshape.239 = f32[896,1280]{1,0:T(8,128)} reshape(f32[56,20480]{1,0:T(8,128)} %fusion.2) | data formatting | bytes 9175040 | tf_op jit(solution)/shard_map/convert_element_type | solution.py:14
  75.5 3.7 copy.58
  79.2 2.1 copy-done
  81.3 0.4 multiply_reduce_fusion.2
  81.7 0.7 rsqrt.16
  82.3 0.4 mul.157
  82.7 2.6 copy.62
  85.3 0.5 multiply_convert_fusion
  85.8 2.5 convert_element_type.204
  88.3 8.8 %add_convert_fusion = bf16[896,1920]{1,0:T(8,128)(2,1)S(1)} fusion(bf16[1280,1920]{1,0:T(8,128)(2,1)} %all-gather.2.cloned.1.call-done, f32[1920]{0:T(1024)} %convert_element_type.189, f32[896,1280]{1,0:T(8,128)} %reshape.239, f32[1280]{0:T(1024)S(1)} %convert_element_type.187, f32[896]{0:T(1024)} %rsqrt.16), kind=kOutput, calls=%fused_computation.9 | convolution fusion | flops 4410900480 | bytes 12959744 | tf_op jit(solution)/shard_map/dot_general | solution.py:18
  97.1 7.5 %reshape.231 = bf16[56,16,3,8,80]{4,3,2,1,0:T(8,128)(2,1)} reshape(bf16[896,1920]{1,0:T(8,128)(2,1)S(1)} %add_convert_fusion) | data formatting | bytes 6881280 | tf_op jit(solution)/shard_map/reshape | solution.py:21
  104.6 3.8 fusion.47
  108.4 1.1 fusion.15
  109.5 0.1 copy-done.2
  109.6 6.7 %fusion.49 = (f32[56,8,16]{2,1,0:T(8,128)S(1)}, f32[56,8,16,16]{2,3,1,0:T(8,128)S(1)}) fusion(f32[56,8,16,16]{2,3,1,0:T(8,128)S(1)} %fusion.15, pred[56,16]{1,0:T(8,128)(4,1)S(1)} %copy-done.4), kind=kOutput, calls=%fused_computation.91 | output fusion | flops 688143 | bytes 947072 | tf_op jit(solution)/shard_map/sub | solution.py:34
  116.3 3.2 fusion.14
  119.5 2.4 convolution_bitcast_fusion
  121.9 8.9 %convolution_bitcast_fusion.2 = bf16[56,16,1,8,80]{4,1,3,0,2:T(8,128)(2,1)} fusion(bf16[56,16,1,8,80]{4,3,2,1,0:T(8,128)(2,1)} %copy-done.2, f32[56,8,16,16]{2,3,1,0:T(8,128)} %fusion.14, f32[56,8,16,16]{2,3,1,0:T(8,128)} %copy-done.12, f32[56,8,16]{2,1,0:T(8,128)S(1)} %get-tuple-element.27), kind=kOutput, calls=%fused_computation.29 | convolution fusion | flops 19160080 | bytes 3239936 | tf_op jit(solution)/shard_map/bhqk,bkhe->bqhe/dot_general | solution.py:77
  130.9 8.4 %convolution_bitcast_fusion.1 = bf16[56,16,1,8,80]{4,1,3,0,2:T(8,128)(2,1)} fusion(bf16[56,16,1,8,80]{4,3,2,1,0:T(8,128)(2,1)S(1)} %get-tuple-element.19, f32[56,8,16,16]{2,3,1,0:T(8,128)} %fusion.14, f32[56,8,16,16]{2,3,1,0:T(8,128)} %copy-done.12, f32[56,8,16]{2,1,0:T(8,128)S(1)} %get-tuple-element.27), kind=kOutput, calls=%fused_computation.28 | convolution fusion | flops 19160080 | bytes 3239936 | tf_op jit(solution)/shard_map/bhqk,bqhe->bkhe/dot_general | solution.py:78
  139.3 4.2 %fusion.46 = (bf16[3,8,80]{2,1,0:T(8,128)(2,1)S(1)}, bf16[56,16,3,8,80]{4,1,3,0,2:T(8,128)(2,1)S(1)}) fusion(bf16[56,16,1,8,80]{4,1,3,0,2:T(8,128)(2,1)} %convolution_bitcast_fusion, bf16[56,16,1,8,80]{4,1,3,0,2:T(8,128)(2,1)} %convolution_bitcast_fusion.1, bf16[56,16,1,8,80]{4,1,3,0,2:T(8,128)(2,1)} %convolution_bitcast_fusion.2), kind=kLoop, calls=%fused_computation.88 | loop fusion | flops 5159040 | bytes 6885120 | tf_op jit(solution)/shard_map/reduce_sum | solution.py:87
  143.5 3.8 copy.49
  147.3 7.4 %convert_element_type.205 = bf16[896,1920]{1,0:T(8,128)(2,1)S(1)} reshape(bf16[56,16,3,8,80]{4,3,2,1,0:T(8,128)(2,1)} %copy.49) | data formatting | bytes 6881280 | tf_op jit(solution)/shard_map/convert_element_type | solution.py:81
  154.7 9.2 %convolution_convert_fusion.4 = bf16[1280,1920]{1,0:T(8,128)(2,1)} fusion(bf16[896,1280]{1,0:T(8,128)(2,1)} %convert_element_type.204, bf16[896,1920]{1,0:T(8,128)(2,1)S(1)} %convert_element_type.205), kind=kOutput, calls=%fused_computation.8 | convolution fusion | flops 4406476800 | bytes 10649600 | tf_op jit(solution)/shard_map/dot_general | solution.py:84
  163.9 8.7 %convert_element_type.198 = bf16[56,16,1920]{2,1,0:T(8,128)(2,1)} reshape(bf16[56,16,3,8,80]{4,3,2,1,0:T(8,128)(2,1)} %copy.49) | data formatting | bytes 6881280 | tf_op jit(solution)/shard_map/convert_element_type | solution.py:81
  172.7 12.1 %multiply_reduce_fusion = (bf16[1280]{0:T(1024)(128)(2,1)S(1)}, f32[56,16]{1,0:T(8,128)S(1)}, f32[56,16,1280]{2,1,0:T(8,128)S(1)}) fusion(f32[56,16]{1,0:T(8,128)S(1)} %get-tuple-element.22, f32[7,8,16,1280]{3,2,1,0:T(8,128)} %copy-done, f32[56,16,1280]{2,1,0:T(8,128)} %bitcast.79, f32[1280]{0:T(1024)S(1)} %convert_element_type.187, ...), kind=kOutput, calls=%fused_computation.12 | convolution fusion | flops 4410898432 | bytes 22133248 | tf_op jit(solution)/shard_map/dot_general | solution.py:88
  184.8 1.2 subtract_convert_fusion
  186.0 0.7 copy.59
  186.7 0.9 convolution_convert_fusion
  187.7 2.0 copy.60
  189.6 4.4 %all-to-all-start.2 = ((bf16[32,2,16,1280]{3,2,1,0:T(8,128)(2,1)}), bf16[32,2,16,1280]{3,2,1,0:T(8,128)(2,1)S(1)}, u32[]{:S(2)}, u32[]{:S(2)}) async-start(bf16[32,2,16,1280]{3,2,1,0:T(8,128)(2,1)} %bitcast.86), calls=%async_computation.2 | async-start | bytes 5242880 | tf_op jit(solution)/shard_map/all_to_all | solution.py:156
  195.5 3.5 convolution_bitcast_fusion.3
  199.0 3.5 copy.46
  202.5 4.8 %reshape.232 = f32[896,640]{1,0:T(8,128)} reshape(f32[56,16,8,80]{3,2,1,0:T(8,128)} %copy.46) | data formatting | bytes 4587520 | tf_op jit(solution)/shard_map/reshape | solution.py:40
  207.3 18.8 %all-reduce.5 = (bf16[1920]{0:T(1024)(128)(2,1)S(1)}, bf16[1280]{0:T(1024)(128)(2,1)S(1)}) all-reduce(bf16[1920]{0:T(1024)(128)(2,1)S(1)} %reduce_sum.84, bf16[1280]{0:T(1024)(128)(2,1)S(1)} %get-tuple-element.5), channel_id=3, replica_groups=mesh['dp'=32,'fsdp'=8] {'fsdp'}, use_global_device_ids=true, to_apply=%region_12.13.clone | all-reduce | flops 3200 | bytes 12800
  226.2 2.9 multiply_convert_fusion.4
  229.1 0.9 copy.61
  230.0 0.6 convolution_convert_fusion.3
  230.5 1.5 reshape_reshape.7
  232.0 140.2 %all-reduce.8 = (f32[160,1920]{1,0:T(8,128)S(1)}, f32[240]{0:T(256)S(1)}, f32[160]{0:T(256)S(1)}) all-reduce(bf16[160,1920]{1,0:T(8,128)(2,1)} %reduce-scatter.2.cloned.1.call-done, f32[240]{0:T(256)S(1)} %dynamic-slice_convert_fusion.1, f32[160]{0:T(256)S(1)} %dynamic-slice_convert_fusion), channel_id=1, replica_groups=mesh['dp'=32,'fsdp'=8] {'dp'}, use_global_device_ids=true, to_apply=%region_10.11 | all-reduce | flops 307600 | bytes 1846400 | tf_op jit(solution)/shard_map/psum | solution.py:177
  372.2 1.1 broadcast_multiply_fusion
  373.4 0.6 broadcast_multiply_fusion.3
  373.9 0.6 broadcast_multiply_fusion.2
  (65 shorter events, 1.3 us)
Async XLA Ops:
  7.2 81.1 %all-gather.2.cloned.1.call-start = ((), (), s32[]{:S(2)}) async-start(), calls=%async_computation.4 | async-start | bytes 5529600 | tf_op jit(solution)/shard_map/all_gather | solution.py:111
  10.2 13.6 %copy-start.7 = (s32[32]{0:T(128)}, s32[32]{0:T(128)S(1)}, u32[]{:S(2)}) copy-start(s32[32]{0:T(128)S(1)} %multiply_add_fusion) | copy-start | bytes 388
  11.8 14.6 %all-to-all-start = ((bf16[32,2,1]{1,2,0:T(2,128)(2,1)}), bf16[32,2,1]{1,2,0:T(2,128)(2,1)S(1)}, u32[]{:S(2)}, u32[]{:S(2)}) async-start(bf16[32,2,1]{1,2,0:T(2,128)(2,1)} %reshape.255), calls=%async_computation | async-start | bytes 32768 | tf_op jit(solution)/shard_map/all_to_all | solution.py:137
  23.8 7.6 %copy-start.9 = (u32[256]{0:T(256)S(1)}, u32[256]{0:T(256)}, u32[]{:S(2)}) copy-start(u32[256]{0:T(256)} %constant.44) | copy-start | bytes 3076
  23.8 9.5 %copy-start.10 = (bf16[160]{0:T(256)(128)(2,1)S(1)}, bf16[160]{0:T(256)(128)(2,1)}, u32[]{:S(2)}) copy-start(bf16[160]{0:T(256)(128)(2,1)} %param.12) | copy-start | bytes 964
  23.8 9.8 %copy-start.11 = (bf16[240]{0:T(256)(128)(2,1)S(1)}, bf16[240]{0:T(256)(128)(2,1)}, u32[]{:S(2)}) copy-start(bf16[240]{0:T(256)(128)(2,1)} %param.11) | copy-start | bytes 1444
  26.4 39.6 %all-to-all-start.1 = ((bf16[32,2,16,1280]{3,2,1,0:T(8,128)(2,1)}), bf16[32,2,16,1280]{3,2,1,0:T(8,128)(2,1)S(1)}, u32[]{:S(2)}, u32[]{:S(2)}) async-start(bf16[32,2,16,1280]{3,2,1,0:T(8,128)(2,1)} %bitcast.21), calls=%async_computation.1 | async-start | bytes 5242880 | tf_op jit(solution)/shard_map/all_to_all | solution.py:136
  31.4 200.6 %reduce-scatter.2.cloned.1.call-start = ((), (), s32[]{:S(2)}) async-start(), calls=%async_computation.5 | async-start | bytes 5529600 | tf_op jit(solution)/shard_map/reduce_scatter | solution.py:167
  57.8 11.9 %copy-start.5 = (pred[64]{0:T(512)(128)(4,1)}, pred[64]{0:T(512)(128)(4,1)S(1)}, u32[]{:S(2)}) copy-start(pred[64]{0:T(512)(128)(4,1)S(1)} %fusion.39) | copy-start | bytes 196
  79.2 2.1 copy-start
  82.3 3.0 slice-start
  82.7 2.6 slice-start.1
  108.4 1.3 copy-start.2
  108.4 7.9 %copy-start.3 = (bf16[56,16,1,8,80]{4,3,2,1,0:T(8,128)(2,1)}, bf16[56,16,1,8,80]{4,3,2,1,0:T(8,128)(2,1)S(1)}, u32[]{:S(2)}) copy-start(bf16[56,16,1,8,80]{4,3,2,1,0:T(8,128)(2,1)S(1)} %get-tuple-element.20) | copy-start | bytes 3440644
  108.4 1.2 copy-start.4
  109.6 6.7 %copy-start.1 = (bf16[56,16,8,80]{3,2,1,0:T(8,128)(2,1)S(1)}, bf16[56,16,8,80]{3,2,1,0:T(8,128)(2,1)}, u32[]{:S(2)}) copy-start(bf16[56,16,8,80]{3,2,1,0:T(8,128)(2,1)} %reshape.233) | copy-start | bytes 3440644
  116.3 3.2 copy-start.12
  116.3 14.6 %copy-start.13 = (f32[56,8,16]{2,1,0:T(8,128)}, f32[56,8,16]{2,1,0:T(8,128)S(1)}, u32[]{:S(2)}) copy-start(f32[56,8,16]{2,1,0:T(8,128)S(1)} %get-tuple-element.27) | copy-start | bytes 86020
  163.9 20.9 %slice-start.2 = ((s8[4587520]{0:T(1024)(128)(4,1)}), s8[393216]{0:T(1024)(128)(4,1)S(1)}, s32[]{:S(2)}) async-start(s8[4587520]{0:T(1024)(128)(4,1)} %bitcast.80), calls=%async_computation.8 | async-start | bytes 786432
  172.7 12.1 %slice-start.3 = ((s8[4587520]{0:T(1024)(128)(4,1)}), s8[4194304]{0:T(1024)(128)(4,1)S(1)}, s32[]{:S(2)}) async-start(s8[4587520]{0:T(1024)(128)(4,1)} %bitcast.80), calls=%async_computation.9 | async-start | bytes 8388608
  186.0 0.8 copy-start.6
  189.6 5.8 %copy-start.14 = (f32[56,8,16]{2,1,0:T(8,128)S(1)}, f32[56,8,16]{2,1,0:T(8,128)}, u32[]{:S(2)}) copy-start(f32[56,8,16]{2,1,0:T(8,128)} %copy-done.13) | copy-start | bytes 86020
  189.6 39.4 %all-to-all-start.2 = ((bf16[32,2,16,1280]{3,2,1,0:T(8,128)(2,1)}), bf16[32,2,16,1280]{3,2,1,0:T(8,128)(2,1)S(1)}, u32[]{:S(2)}, u32[]{:S(2)}) async-start(bf16[32,2,16,1280]{3,2,1,0:T(8,128)(2,1)} %bitcast.86), calls=%async_computation.2 | async-start | bytes 5242880 | tf_op jit(solution)/shard_map/all_to_all | solution.py:156
  226.2 3.7 copy-start.8
Sparse Core Ops, SparseCore 0:
  9.8 62.9 all-gather.1
  164.0 59.6 reduce-scatter.1
where the time goes:
time: 388 us; the launch traced here: 382 us
  blocking collectives  177 us (46%)
  local copies, waits for them, and re-layouts  73.5 us (19%)
  matrix products  63.7 us (16%)
  other arithmetic  22.2 us (6%)
  between operations  17.3 us (4%)
  starting transfers between devices  16.8 us (4%)
  waiting for transfers between devices  10.6 us (3%)
    psum x1, blocking collectives, local(): lax.psum((shard_sums[0], shard_sums[1], shard_sums[2]), 'dp')  140 us
    unnamed x2, blocking collectives  37.2 us
    convert_element_type x3, local copies, waits for them, and re-layouts, backward(): d_packed = jnp.stack([d_query, d_keys, d_values], axis=2).astype(jnp.bflo...  19.9 us
    unnamed x50, local copies, waits for them, and re-layouts  16.1 us
    dot_general x1, matrix products, backward(): lax.dot_general(d_packed, weight, (((1,), (1,)), ((), ())), preferred_ele...  12.1 us
    dot_general x1, matrix products, backward(): lax.dot_general(normed_flat, d_packed, (((0,), (0,)), ((), ())), preferre...  9.23 us
    dot_general x1, matrix products, backward(): jnp.einsum('bhqk,bkhe->bqhe', d_scores_b, keyset, preferred_element_type=...  8.94 us
    dot_general x1, matrix products, forward(): jnp.dot(normed_flat, weight, preferred_element_type=jnp.float32)  8.77 us
  transfers between devices with their start and end apart: 5, of which 2 were waited for; matrix products, arithmetic and copies ran while one was open for 21% of the time, Pallas kernels for 0%

commit v1 on v0

v1 whole, which is shorter than its diff:
```python
import functools
import math

import jax
import jax.numpy as jnp
from jax import lax
from jax.experimental import pallas as pl
from jax.experimental.pallas import tpu as pltpu
from jax.sharding import PartitionSpec as P

MESH = pl.DeviceIdType.MESH
BF = jnp.bfloat16
F32 = jnp.float32
D = 1280
QKV = 1920
HEADS = 8
HD = 80
W3 = HEADS * HD
SLOT = 16
IMG = 32
ROWS = IMG * SLOT
RECV = 56
NDP = 32
NZ = 8
CHIPS = 16
SHARD = D // NZ
HALF = SHARD // 2
PIECES = 16
LIMIT = 58 * 2**20
COLS = ((0, 512), (512, 512), (1024, 512), (1536, 384))
VM = pl.BlockSpec(memory_space=pltpu.VMEM)
SM = pl.BlockSpec(memory_space=pltpu.SMEM)


def params(cid=None):
    if cid is None:
        return pltpu.CompilerParams(vmem_limit_bytes=LIMIT)
    return pltpu.CompilerParams(vmem_limit_bytes=LIMIT, collective_id=cid, has_side_effects=True)


def remote(src, dst, send, recv, where):
    return pltpu.make_async_remote_copy(
        src_ref=src, dst_ref=dst, send_sem=send, recv_sem=recv, device_id=where, device_id_type=MESH
    )


def table_kernel(dest_ref, lane_ref, cnt_ref, seen):
    def clear(e, _):
        seen[e] = 0
        return 0

    lax.fori_loop(0, NDP, clear, 0)

    def place(i, _):
        e = dest_ref[i]
        k = seen[e]
        lane_ref[i] = 2 * e + jnp.minimum(k, 1)
        seen[e] = k + 1
        return 0

    lax.fori_loop(0, IMG, place, 0)

    def spread(e, _):
        cnt_ref[e] = jnp.full((8, 128), seen[e], jnp.int32)
        return 0

    lax.fori_loop(0, NDP, spread, 0)


def tables(destination):
    return pl.pallas_call(
        table_kernel,
        out_shape=(
            jax.ShapeDtypeStruct((IMG,), jnp.int32),
            jax.ShapeDtypeStruct((NDP, 8, 128), jnp.int32),
        ),
        in_specs=[SM],
        out_specs=(SM, VM),
        scratch_shapes=[pltpu.SMEM((NDP,), jnp.int32)],
        compiler_params=params(),
    )(destination)


def gather_kernel(
    w_ref, small_ref, cnt_ref, grad_ref,
    wf_ref, params_ref, garr_ref, counts_ref,
    small_all, cbuf, stage, cvec, csm, starts,
    c_send, c_recv, g_send, g_recv, s_send, s_recv, r_send, r_recv, b_send, b_recv, l_sem,
):
    me = lax.axis_index("dp")
    z = lax.axis_index("fsdp")
    core = lax.rem(me, 2)
    sib = me + 1 - 2 * core

    barrier = pltpu.get_barrier_semaphore()

    def greet(k, _):
        pl.semaphore_signal(barrier, inc=1, device_id={"dp": lax.rem(me + k, NDP)}, device_id_type=MESH)
        return 0

    lax.fori_loop(1, NDP, greet, 0)
    for k in range(1, NZ):
        pl.semaphore_signal(barrier, inc=1, device_id={"fsdp": lax.rem(z + k, NZ)}, device_id_type=MESH)
    pl.semaphore_wait(barrier, NDP - 1 + NZ - 1)

    def count_copy(k):
        peer = lax.rem(me + k, NDP)
        return remote(cnt_ref.at[peer], cbuf.at[me], c_send.at[k], c_recv.at[me], {"dp": peer})

    def count_start(k, _):
        count_copy(k).start()
        return 0

    lax.fori_loop(1, NDP, count_start, 0)

    def rows_of(t):
        return pl.ds(pl.multiple_of(t * SHARD + core * HALF, 16), HALF)

    def ring_valid(d, s, q):
        return s < 3 or (s == 3 and (q < 2) == (d == 0))

    def ring_copy(d, s, q):
        cols = pl.ds(*COLS[q])
        if d == 0:
            t, to = lax.rem(z - s + NZ, NZ), lax.rem(z + 1, NZ)
        else:
            t, to = lax.rem(z + s, NZ), lax.rem(z + NZ - 1, NZ)
        dst = wf_ref.at[rows_of(t), cols]
        src = w_ref.at[pl.ds(pl.multiple_of(core * HALF, 16), HALF), cols] if s == 0 else dst
        return remote(src, dst, r_send.at[d, s, q], r_recv.at[d, s, q], {"fsdp": to})

    def arrived_from(d, s):
        return lax.rem(z - 1 - s + NZ, NZ) if d == 0 else lax.rem(z + 1 + s, NZ)

    def sib_copy(d, s, q):
        block = wf_ref.at[rows_of(arrived_from(d, s)), pl.ds(*COLS[q])]
        return remote(block, block, b_send.at[d, s, q], b_recv.at[d, s, q], {"dp": sib})

    for q in range(4):
        for d in range(2):
            ring_copy(d, 0, q).start()

    def small_copy(k):
        to = lax.rem(z + k, NZ)
        return remote(small_ref, small_all.at[z], s_send.at[k], s_recv.at[z], {"fsdp": to})

    for k in range(1, NZ):
        small_copy(k).start()
    small_all[z] = small_ref[...]
    wf_ref[pl.ds(pl.multiple_of(z * SHARD, 16), SHARD), :] = w_ref[...]

    cbuf[me] = cnt_ref[me]

    def count_wait(k, _):
        src = lax.rem(me + k, NDP)
        remote(cnt_ref.at[src], cbuf.at[src], c_send.at[k], c_recv.at[src], {"dp": src}).wait()
        return 0

    lax.fori_loop(1, NDP, count_wait, 0)
    lane = lax.broadcasted_iota(jnp.int32, (8, 128), 1)
    total = jnp.zeros((8, 128), jnp.int32)
    for s in range(NDP):
        total = total + jnp.where(lane == s, cbuf[s], 0)
    cvec[...] = total
    counts_ref[...] = total
    to_smem = pltpu.make_async_copy(cvec, csm, l_sem)
    to_smem.start()
    to_smem.wait()

    def prefix(s, start):
        starts[s] = start
        return start + csm[0, s]

    lax.fori_loop(0, NDP, prefix, jnp.int32(0))

    def grad_copy(k):
        peer = lax.rem(me + k, NDP)
        return remote(stage.at[peer], garr_ref.at[me], g_send.at[k], g_recv.at[me], {"dp": peer})

    def grad_start(k, _):
        peer = lax.rem(me + k, NDP)
        first = jnp.minimum(starts[peer], RECV - 1)
        second = jnp.minimum(first + 1, RECV - 1)
        stage[peer, 0] = grad_ref[first]
        stage[peer, 1] = grad_ref[second]
        grad_copy(k).start()
        return 0

    lax.fori_loop(1, NDP, grad_start, 0)
    first = jnp.minimum(starts[me], RECV - 1)
    garr_ref[me, 0] = grad_ref[first]
    garr_ref[me, 1] = grad_ref[jnp.minimum(first + 1, RECV - 1)]

    for s in range(4):
        for q in range(4):
            for d in range(2):
                if ring_valid(d, s, q):
                    ring_copy(d, s, q).wait_recv()
                    if ring_valid(d, s + 1, q):
                        ring_copy(d, s + 1, q).start()
                    sib_copy(d, s, q).start()

    for k in range(1, NZ):
        src = lax.rem(z + k, NZ)
        remote(small_ref, small_all.at[src], s_send.at[k], s_recv.at[src], {"fsdp": src}).wait()
    got = jnp.zeros((32, 128), F32)
    for s in range(NZ):
        got = got + small_all[s].astype(F32)
    params_ref[...] = got

    for s in range(4):
        for q in range(4):
            for d in range(2):
                if ring_valid(d, s, q):
                    ring_copy(d, s, q).wait_send()
                    sib_copy(d, s, q).wait()

    def grad_wait(k, _):
        src = lax.rem(me + k, NDP)
        remote(stage.at[src], garr_ref.at[src], g_send.at[k], g_recv.at[src], {"dp": src}).wait()
        return 0

    lax.fori_loop(1, NDP, grad_wait, 0)


def gather(weight, small, cnt, grad):
    dma = pltpu.SemaphoreType.DMA
    return pl.pallas_call(
        gather_kernel,
        out_shape=(
            jax.ShapeDtypeStruct((D, QKV), BF),
            jax.ShapeDtypeStruct((32, 128), F32),
            jax.ShapeDtypeStruct((NDP, 2, SLOT, W3), BF),
            jax.ShapeDtypeStruct((8, 128), jnp.int32),
        ),
        in_specs=[VM] * 4,
        out_specs=(VM,) * 4,
        scratch_shapes=[
            pltpu.VMEM((NZ, 32, 128), BF),
            pltpu.VMEM((NDP, 8, 128), jnp.int32),
            pltpu.VMEM((NDP, 2, SLOT, W3), BF),
            pltpu.VMEM((8, 128), jnp.int32),
            pltpu.SMEM((8, 128), jnp.int32),
            pltpu.SMEM((NDP,), jnp.int32),
            dma((NDP,)), dma((NDP,)), dma((NDP,)), dma((NDP,)), dma((NZ,)), dma((NZ,)),
            dma((2, 4, 4)), dma((2, 4, 4)), dma((2, 4, 4)), dma((2, 4, 4)), dma,
        ],
        compiler_params=params(1),
    )(weight, small, cnt, grad)


def dot_nn(a, b):
    return lax.dot_general(a, b, (((1,), (0,)), ((), ())), preferred_element_type=F32)


def dot_nt(a, b):
    return lax.dot_general(a, b, (((1,), (1,)), ((), ())), preferred_element_type=F32)


def window(h):
    low = (HD * h // 128) * 128
    high = -(-(HD * h + HD) // 128) * 128
    return low, high - low


def compute_kernel(
    lane_ref, x_ref, w_ref, par_ref, valid_ref, garr_ref,
    dx_ref, lanes_ref, p_ref,
    normed, normed_t, qkv, dqkv, g, att, dn, inv, row, dgain, small,
):
    for i in range(15):
        row[0:1, 128 * i : 128 * i + 128] = par_ref[i : i + 1, :]
    for i in range(10):
        row[1:2, 128 * i : 128 * i + 128] = par_ref[15 + i : 16 + i, :]

    def norm_block(b, _):
        rows = pl.ds(pl.multiple_of(b * 128, 128), 128)
        x = x_ref[rows, :].astype(F32)
        r = lax.rsqrt(jnp.mean(x * x, axis=-1, keepdims=True) + 1e-06)
        inv[rows, :] = jnp.broadcast_to(r, (128, 128))
        y = x * r * row[1:2, 0:D]
        normed[rows, :] = y.astype(BF)
        normed_t[:, rows] = y.T.astype(BF)
        return 0

    lax.fori_loop(0, 4, norm_block, 0)

    def project(n, _):
        cols = pl.ds(pl.multiple_of(n * 384, 128), 384)
        for m in range(2):
            r = dot_nn(normed[256 * m : 256 * m + 256, :], w_ref[:, cols]) + row[0:1, cols]
            qkv[256 * m : 256 * m + 256, cols] = r.astype(BF)
        return 0

    lax.fori_loop(0, 5, project, 0)

    def take_grad(i, _):
        g[pl.ds(pl.multiple_of(i * SLOT, SLOT), SLOT), :] = garr_ref[lane_ref[i]]
        return 0

    lax.fori_loop(0, IMG, take_grad, 0)

    dqkv[...] = jnp.zeros_like(dqkv)
    att[...] = jnp.zeros_like(att)
    scale = 1.0 / math.sqrt(HD)
    same = (
        lax.broadcasted_iota(jnp.int32, (128, 128), 0) // SLOT
        == lax.broadcasted_iota(jnp.int32, (128, 128), 1) // SLOT
    )

    def attend(b, _):
        rows = pl.ds(pl.multiple_of(b * 128, 128), 128)
        valid = jnp.broadcast_to(valid_ref[pl.ds(b, 1), :], (128, 128))
        keys = same & (valid > 0.5)
        live = valid.T
        for h in range(HEADS):
            low, width = window(h)
            col = lax.broadcasted_iota(jnp.int32, (128, width), 1) + low
            mine = (col >= HD * h) & (col < HD * h + HD)
            livew = live[:, :1] > 0.5
            zero = jnp.zeros((128, width), BF)
            q = jnp.where(mine, qkv[rows, low : low + width], zero)
            k = jnp.where(mine, qkv[rows, W3 + low : W3 + low + width], zero)
            v = jnp.where(mine, qkv[rows, 2 * W3 + low : 2 * W3 + low + width], zero)
            gh = jnp.where(mine & livew, g[rows, low : low + width], zero)
            s = jnp.where(keys, dot_nt(q, k) * scale, -1e30)
            e = jnp.exp(s - jnp.max(s, axis=-1, keepdims=True))
            p = e / jnp.sum(e, axis=-1, keepdims=True)
            o = jnp.where(livew, dot_nn(p.astype(BF), v), 0.0)
            dp = dot_nt(gh, v)
            ds = p * (dp - jnp.sum(dp * p, axis=-1, keepdims=True)) * scale
            dv = dot_nn(p.T.astype(BF), gh)
            dq = dot_nn(ds.astype(BF), k)
            dk = dot_nn(ds.T.astype(BF), q)
            att[rows, low : low + width] += o.astype(BF)
            dqkv[rows, low : low + width] += dq.astype(BF)
            dqkv[rows, W3 + low : W3 + low + width] += dk.astype(BF)
            dqkv[rows, 2 * W3 + low : 2 * W3 + low + width] += dv.astype(BF)
        return 0

    lax.fori_loop(0, 4, attend, 0)

    lanes_ref[...] = jnp.zeros_like(lanes_ref)

    def put_lane(i, _):
        lanes_ref[lane_ref[i]] = att[pl.ds(pl.multiple_of(i * SLOT, SLOT), SLOT), :]
        return 0

    lax.fori_loop(0, IMG, put_lane, 0)

    def weight_grad(j, _):
        left = normed_t[pl.ds(pl.multiple_of(j * 320, 64), 320), :]
        for k in range(3):
            r = dot_nn(left, dqkv[:, 640 * k : 640 * k + 640]).astype(BF)
            p_ref[pl.ds(4 * j, 4), 5 * k : 5 * k + 5] = r.reshape(4, 5, SLOT, 640)
        return 0

    lax.fori_loop(0, 4, weight_grad, 0)

    def input_grad(n, _):
        cols = pl.ds(pl.multiple_of(n * 256, 256), 256)
        for m in range(2):
            dn[256 * m : 256 * m + 256, cols] = dot_nt(dqkv[256 * m : 256 * m + 256, :], w_ref[cols, :])
        return 0

    lax.fori_loop(0, 5, input_grad, 0)

    dgain[...] = jnp.zeros_like(dgain)

    def finish(b, _):
        rows = pl.ds(pl.multiple_of(b * 32, 32), 32)
        x = x_ref[rows, :].astype(F32)
        r = inv[rows, 0:1]
        d = dn[rows, :]
        scaled = d * row[1:2, 0:D]
        m = jnp.mean(scaled * x, axis=-1, keepdims=True)
        dx_ref[rows, :] = (r * scaled - x * (r * r * r) * m).astype(BF)
        t = d * x * r
        dgain[:, 0:D] += t[0:8] + t[8:16] + t[16:24] + t[24:32]
        return 0

    lax.fori_loop(0, 16, finish, 0)

    def bias_sum(b, acc):
        t = dqkv[pl.ds(pl.multiple_of(b * 32, 32), 32), :].astype(F32)
        return acc + (t[0:8] + t[8:16] + t[16:24] + t[24:32])

    db = jnp.sum(lax.fori_loop(0, 16, bias_sum, jnp.zeros((8, QKV), F32)), axis=0, keepdims=True)
    dg = jnp.sum(dgain[:, 0:D], axis=0, keepdims=True)
    small[...] = jnp.zeros_like(small)
    for i in range(3):
        small[i : i + 1, :] = db[:, 640 * i : 640 * i + 640]
    for i in range(2):
        small[3 + i : 4 + i, :] = dg[:, 640 * i : 640 * i + 640]
    tile = small[...].astype(BF)
    for i in range(2 * NZ):
        p_ref[i, PIECES - 1] = tile


def compute(lane, x, weight, par, valid, garr):
    return pl.pallas_call(
        compute_kernel,
        out_shape=(
            jax.ShapeDtypeStruct((ROWS, D), BF),
            jax.ShapeDtypeStruct((2 * NDP, SLOT, W3), BF),
            jax.ShapeDtypeStruct((2 * NZ, PIECES, SLOT, 640), BF),
        ),
        in_specs=[SM] + [VM] * 5,
        out_specs=(VM,) * 3,
        scratch_shapes=[
            pltpu.VMEM((ROWS, D), BF),
            pltpu.VMEM((D, ROWS), BF),
            pltpu.VMEM((ROWS, QKV), BF),
            pltpu.VMEM((ROWS, QKV), BF),
            pltpu.VMEM((ROWS, W3), BF),
            pltpu.VMEM((ROWS, W3), BF),
            pltpu.VMEM((ROWS, D), F32),
            pltpu.VMEM((ROWS, 128), F32),
            pltpu.VMEM((8, QKV), F32),
            pltpu.VMEM((8, D), F32),
            pltpu.VMEM((16, 640), F32),
        ],
        compiler_params=params(),
    )(lane, x, weight, par, valid, garr)


def reduce_kernel(
    p_ref, lanes_ref,
    fin_ref, att_ref,
    pair, ring_in, ring_out, total, plane,
    a_send, a_recv, p_send, p_recv, r_send, r_recv, x_send, x_recv, y_send, y_recv, f_send, f_recv,
):
    me = lax.axis_index("dp")
    z = lax.axis_index("fsdp")
    core = lax.rem(me, 2)
    chip = me // 2
    sib = me + 1 - 2 * core
    ahead, behind = lax.rem(z + 1, NZ), lax.rem(z + NZ - 1, NZ)

    barrier = pltpu.get_barrier_semaphore()

    def greet(k, _):
        pl.semaphore_signal(barrier, inc=1, device_id={"dp": lax.rem(me + k, NDP)}, device_id_type=MESH)
        return 0

    lax.fori_loop(1, NDP, greet, 0)
    for to in (ahead, behind):
        pl.semaphore_signal(barrier, inc=1, device_id={"fsdp": to}, device_id_type=MESH)
    pl.semaphore_wait(barrier, NDP - 1 + 2)

    def target(off):
        return lax.rem(z + off + NZ, NZ)

    def pair_copy(off):
        t = target(off)
        return remote(p_ref.at[2 * t + 1 - core], pair.at[t], p_send.at[off + 3], p_recv.at[off + 3], {"dp": sib})

    for off in (4, 3, -3, 2, -2, 1, -1, 0):
        pair_copy(off).start()

    def att_copy(k):
        peer = lax.rem(me + k, NDP)
        return remote(lanes_ref.at[peer], att_ref.at[me], a_send.at[k], a_recv.at[me], {"dp": peer})

    def att_start(k, _):
        att_copy(k).start()
        return 0

    lax.fori_loop(1, NDP, att_start, 0)
    att_ref[me] = lanes_ref[me]

    def ring_valid(d, s, q):
        return s > 0 or (q < 2) == (d == 0)

    def ring_copy(d, s, q):
        part = pl.ds(4 * q, 4)
        return remote(
            ring_out.at[d, s, part], ring_in.at[d, s, part], r_send.at[d, s, q], r_recv.at[d, s, q],
            {"fsdp": behind if d else ahead},
        )

    def mine(off, q):
        t = target(off)
        part = pl.ds(4 * q, 4)
        return p_ref[2 * t + core, part].astype(F32) + pair[t, part].astype(F32)

    for s in range(4):
        for d in range(2):
            off = 4 - s if d == 0 else s - 4
            if s == 0:
                off = 4
            if s > 0 or d == 0:
                pair_copy(off).wait_recv()
        for q in range(4):
            for d in range(2):
                off = 4 - s if d == 0 else s - 4
                if s == 0:
                    off = 4
                if ring_valid(d, s, q):
                    r = mine(off, q)
                    if s > 0 and ring_valid(d, s - 1, q):
                        ring_copy(d, s - 1, q).wait_recv()
                        r = r + ring_in[d, s - 1, pl.ds(4 * q, 4)].astype(F32)
                    ring_out[d, s, pl.ds(4 * q, 4)] = r.astype(BF)
                    ring_copy(d, s, q).start()
    pair_copy(0).wait_recv()
    for q in range(4):
        r = mine(0, q)
        for d in range(2):
            ring_copy(d, 3, q).wait_recv()
            r = r + ring_in[d, 3, pl.ds(4 * q, 4)].astype(F32)
        total[pl.ds(4 * q, 4)] = r.astype(BF)

    def scatter_copy(k):
        i = lax.rem(chip + k, CHIPS)
        return remote(total.at[i], plane.at[chip], x_send.at[k], x_recv.at[chip], {"dp": 2 * i + core})

    def scatter_start(k, _):
        scatter_copy(k).start()
        return 0

    lax.fori_loop(1, CHIPS, scatter_start, 0)
    plane[chip] = total[chip]

    def scatter_wait(k, _):
        i = lax.rem(chip + k, CHIPS)
        remote(total.at[i], plane.at[i], x_send.at[k], x_recv.at[i], {"dp": 2 * i + core}).wait()
        return 0

    lax.fori_loop(1, CHIPS, scatter_wait, 0)
    r = jnp.zeros((SLOT, 640), F32)
    for i in range(CHIPS):
        r = r + plane[i].astype(F32)
    fin_ref[core, chip] = r.astype(BF)

    def share_copy(k, slot):
        i = lax.rem(chip + k, CHIPS)
        return remote(
            fin_ref.at[core, slot], fin_ref.at[core, slot], y_send.at[k], y_recv.at[slot], {"dp": 2 * i + core}
        )

    def share_start(k, _):
        share_copy(k, chip).start()
        return 0

    lax.fori_loop(1, CHIPS, share_start, 0)

    def share_wait(k, _):
        i = lax.rem(chip + k, CHIPS)
        share_copy(k, i).wait_recv()
        return 0

    lax.fori_loop(1, CHIPS, share_wait, 0)
    last = remote(fin_ref.at[core], fin_ref.at[core], f_send, f_recv, {"dp": sib})
    last.start()

    def share_sent(k, _):
        share_copy(k, chip).wait_send()
        return 0

    lax.fori_loop(1, CHIPS, share_sent, 0)
    for off in (4, 3, -3, 2, -2, 1, -1, 0):
        pair_copy(off).wait_send()
    for s in range(4):
        for q in range(4):
            for d in range(2):
                if ring_valid(d, s, q):
                    ring_copy(d, s, q).wait_send()

    def att_wait(k, _):
        src = lax.rem(me + k, NDP)
        remote(lanes_ref.at[src], att_ref.at[src], a_send.at[k], a_recv.at[src], {"dp": src}).wait()
        return 0

    lax.fori_loop(1, NDP, att_wait, 0)
    last.wait()


def reduce(pieces, lanes):
    dma = pltpu.SemaphoreType.DMA
    return pl.pallas_call(
        reduce_kernel,
        out_shape=(
            jax.ShapeDtypeStruct((2, PIECES, SLOT, 640), BF),
            jax.ShapeDtypeStruct((NDP, 2, SLOT, W3), BF),
        ),
        in_specs=[VM] * 2,
        out_specs=(VM,) * 2,
        scratch_shapes=[
            pltpu.VMEM((NZ, PIECES, SLOT, 640), BF),
            pltpu.VMEM((2, 4, PIECES, SLOT, 640), BF),
            pltpu.VMEM((2, 4, PIECES, SLOT, 640), BF),
            pltpu.VMEM((PIECES, SLOT, 640), BF),
            pltpu.VMEM((CHIPS, SLOT, 640), BF),
            dma((NDP,)), dma((NDP,)), dma((NZ,)), dma((NZ,)), dma((2, 4, 4)), dma((2, 4, 4)),
            dma((CHIPS,)), dma((CHIPS,)), dma((CHIPS,)), dma((CHIPS,)), dma, dma,
        ],
        compiler_params=params(2),
    )(pieces, lanes)


def finish_kernel(counts_ref, fin_ref, arr_ref, att_ref, gw_ref, small_ref):
    scale = 1.0 / math.sqrt(NDP * NZ * ROWS)
    att_ref[...] = jnp.zeros_like(att_ref)

    def place(src, start):
        n = counts_ref[0, src]
        for k in range(2):

            @pl.when(n > k)
            def _():
                att_ref[jnp.minimum(start + k, RECV - 1)] = arr_ref[2 * src + k]

        return start + n

    lax.fori_loop(0, NDP, place, jnp.int32(0))
    for c in range(2):
        for i in range(PIECES - 1):
            r0, c0 = HALF * c + SLOT * (i % 5), 640 * (i // 5)
            gw_ref[r0 : r0 + SLOT, c0 : c0 + 640] = fin_ref[c, i].astype(F32) * scale
    small_ref[...] = fin_ref[0, PIECES - 1].astype(F32) * scale


def finish(counts, fin, arr):
    return pl.pallas_call(
        finish_kernel,
        out_shape=(
            jax.ShapeDtypeStruct((RECV, SLOT, W3), BF),
            jax.ShapeDtypeStruct((SHARD, QKV), F32),
            jax.ShapeDtypeStruct((SLOT, 640), F32),
        ),
        in_specs=[SM, VM, VM],
        out_specs=(VM,) * 3,
        compiler_params=params(),
    )(counts, fin, arr)


def local(patches, patch_count, destination, qkv_weight, qkv_bias, norm_gain, grad_out):
    z = lax.axis_index("fsdp")
    small = jnp.zeros((4096,), BF)
    small = lax.dynamic_update_slice(small, qkv_bias, (z * (QKV // NZ),))
    small = lax.dynamic_update_slice(small, norm_gain, (QKV + z * SHARD,)).reshape(32, 128)
    valid = (jnp.arange(SLOT)[None, :] < jnp.maximum(patch_count, 1)[:, None]).astype(F32).reshape(4, 128)
    lane, cnt = tables(destination)
    weight, par, garr, counts = gather(qkv_weight, small, cnt, grad_out.reshape(RECV, SLOT, W3))
    dx, lanes, pieces = compute(lane, patches, weight, par, valid, garr.reshape(2 * NDP, SLOT, W3))
    fin, arr = reduce(pieces, lanes.reshape(NDP, 2, SLOT, W3))
    att, gw, sums = finish(counts, fin, arr.reshape(2 * NDP, SLOT, W3))
    gb = lax.dynamic_slice(sums[0:3].reshape(QKV), (z * (QKV // NZ),), (QKV // NZ,))
    gg = lax.dynamic_slice(sums[3:5].reshape(D), (z * SHARD,), (SHARD,))
    return att.reshape(RECV * SLOT, W3), dx, gw, gb, gg


def solution(mesh):
    return jax.shard_map(
        local,
        mesh=mesh,
        in_specs=(
            P(("dp", "fsdp"), None),
            P(("dp", "fsdp")),
            P(("dp", "fsdp")),
            P("fsdp", None),
            P("fsdp"),
            P("fsdp"),
            P(("dp", "fsdp"), None),
        ),
        out_specs=(
            P(("dp", "fsdp"), None),
            P(("dp", "fsdp"), None),
            P("fsdp", None),
            P("fsdp"),
            P("fsdp"),
        ),
        check_vma=False,
    )
```

time: 388 us -> 152 us (0.39)
  the two profiles are of different devices: /device:TPU:32 before, /device:TPU:1 now
where the time goes in v1:
time: 152 us
  Pallas kernels  145 us (95%)
  local copies, waits for them, and re-layouts  4.77 us (3%)
    pallas_call x1, Pallas kernels, reduce(): pl.pallas_call(reduce_kernel, out_shape=(jax.ShapeDtypeStruct((2, PIECES,...  52.3 us
    pallas_call x1, Pallas kernels, gather(): pl.pallas_call(gather_kernel, out_shape=(jax.ShapeDtypeStruct((D, QKV), B...  46.9 us
    pallas_call x1, Pallas kernels, compute(): pl.pallas_call(compute_kernel, out_shape=(jax.ShapeDtypeStruct((ROWS, D),...  40.4 us
    pallas_call x1, Pallas kernels, finish(): pl.pallas_call(finish_kernel, out_shape=(jax.ShapeDtypeStruct((RECV, SLOT...  3.75 us

profile of v1, /device:TPU:1, one launch (start us, length us, event | category | flops | bytes accessed | tf_op | source)
XLA Modules:
  0.0 152.0 jit_solution(5872823208533824599)
XLA Ops:
  0.6 0.7 broadcast_maximum_fusion
  1.3 0.1 lt.37
  1.4 0.1 lt.35
  1.5 0.9 dynamic_update_slice.6
  2.3 0.8 dynamic_update_slice.7
  3.2 0.0 copy-start
  3.2 0.1 lt.38
  3.2 0.1 lt.39
  3.3 0.6 compare_convert_fusion.valid_ref
  3.9 2.0 %shard_map.110 = (s32[32]{0:T(128)}, s32[32,8,128]{2,1,0:T(8,128)}) custom-call(s32[32]{0:T(128)} %dest_ref.1), custom_call_target="tpu_custom_call" | custom-call | tf_op jit(solution)/shard_map/pallas_call | solution.py:71
  5.9 0.0 copy-done
  5.9 46.9 %shard_map.111 = (bf16[1280,1920]{1,0:T(8,128)(2,1)}, f32[32,128]{1,0:T(8,128)}, bf16[32,2,16,640]{3,2,1,0:T(8,128)(2,1)}, s32[8,128]{1,0:T(8,128)}) custom-call(bf16[160,1920]{1,0:T(8,128)(2,1)} %w_ref.1, bf16[32,128]{1,0:T(8,128)(2,1)} %bitcast.10, s32[32,8,128]{2,1,0:T(8,128)} %get-tuple-element.19.cnt_ref, bf16[56,16,640]{2,1,0:T(8,128)(2,1)} %bitcast.9), custom_call_target="tpu_custom_call" | custom-call | tf_op jit(solution)/shard_map/pallas_call | solution.py:228
  52.8 40.4 %shard_map.112 = (bf16[512,1280]{1,0:T(8,128)(2,1)}, bf16[64,16,640]{2,1,0:T(8,128)(2,1)}, bf16[16,16,16,640]{3,2,1,0:T(8,128)(2,1)}) custom-call(s32[32]{0:T(128)} %get-tuple-element.21.lane_ref, bf16[512,1280]{1,0:T(8,128)(2,1)} %x_ref.1, bf16[1280,1920]{1,0:T(8,128)(2,1)} %get-tuple-element.22.w_ref, f32[32,128]{1,0:T(8,128)} %get-tuple-element.23.par_ref, ...), custom_call_target="tpu_custom_call" | custom-call | tf_op jit(solution)/shard_map/pallas_call | solution.py:401
  93.2 52.3 %shard_map.113 = (bf16[2,16,16,640]{3,2,1,0:T(8,128)(2,1)}, bf16[32,2,16,640]{3,2,1,0:T(8,128)(2,1)}) custom-call(bf16[16,16,16,640]{3,2,1,0:T(8,128)(2,1)} %get-tuple-element.25.p_ref, bf16[32,2,16,640]{3,2,1,0:T(8,128)(2,1)} %bitcast.8), custom_call_target="tpu_custom_call" | custom-call | tf_op jit(solution)/shard_map/pallas_call | solution.py:581
  145.5 3.8 %shard_map.114 = (bf16[56,16,640]{2,1,0:T(8,128)(2,1)}, f32[160,1920]{1,0:T(8,128)}, f32[16,640]{1,0:T(8,128)}) custom-call(s32[8,128]{1,0:T(8,128)} %get-tuple-element.20.counts_ref, bf16[2,16,16,640]{3,2,1,0:T(8,128)(2,1)} %get-tuple-element.27.fin_ref, bf16[64,16,640]{2,1,0:T(8,128)(2,1)} %bitcast.6), custom_call_target="tpu_custom_call" | custom-call | tf_op jit(solution)/shard_map/pallas_call | solution.py:625
  149.2 0.7 slice.7
  149.9 0.7 slice.6
  150.7 0.6 dynamic_slice.6
  151.3 0.6 dynamic_slice.7
  (4 shorter events, 0.0 us)
Async XLA Ops:
  3.2 2.8 %copy-start = (bf16[4096]{0:T(1024)(128)(2,1)}, bf16[4096]{0:T(1024)(128)(2,1)S(1)}, u32[]{:S(2)}) copy-start(bf16[4096]{0:T(1024)(128)(2,1)S(1)} %dynamic_update_slice.7) | copy-start | bytes 24580

commit v2 on v1

v2 whole, which is shorter than its diff:
```python
import functools
import math

import jax
import jax.numpy as jnp
from jax import lax
from jax.experimental import pallas as pl
from jax.experimental.pallas import tpu as pltpu
from jax.sharding import PartitionSpec as P

MESH = pl.DeviceIdType.MESH
BF = jnp.bfloat16
F32 = jnp.float32
D = 1280
QKV = 1920
HEADS = 8
HD = 80
W3 = HEADS * HD
SLOT = 16
IMG = 32
ROWS = IMG * SLOT
RECV = 56
NDP = 32
NZ = 8
CHIPS = 16
SHARD = D // NZ
HALF = SHARD // 2
PIECES = 16
LIMIT = 58 * 2**20
COLS = ((0, 512), (512, 512), (1024, 512), (1536, 384))
VM = pl.BlockSpec(memory_space=pltpu.VMEM)
SM = pl.BlockSpec(memory_space=pltpu.SMEM)


def params(cid=None):
    if cid is None:
        return pltpu.CompilerParams(vmem_limit_bytes=LIMIT)
    return pltpu.CompilerParams(vmem_limit_bytes=LIMIT, collective_id=cid, has_side_effects=True)


def remote(src, dst, send, recv, where):
    return pltpu.make_async_remote_copy(
        src_ref=src, dst_ref=dst, send_sem=send, recv_sem=recv, device_id=where, device_id_type=MESH
    )


def table_kernel(dest_ref, lane_ref, inverse_ref, cnt_ref, seen):
    def clear(e, _):
        seen[e] = 0
        return 0

    lax.fori_loop(0, NDP, clear, 0)

    def clear_lane(n, _):
        inverse_ref[n] = 0
        return 0

    lax.fori_loop(0, 2 * NDP, clear_lane, 0)

    def place(i, _):
        e = dest_ref[i]
        k = seen[e]
        lane_ref[i] = 2 * e + jnp.minimum(k, 1)
        inverse_ref[2 * e + jnp.minimum(k, 1)] = i
        seen[e] = k + 1
        return 0

    lax.fori_loop(0, IMG, place, 0)

    def spread(e, _):
        cnt_ref[e] = jnp.full((8, 128), seen[e], jnp.int32)
        return 0

    lax.fori_loop(0, NDP, spread, 0)


def tables(destination):
    return pl.pallas_call(
        table_kernel,
        out_shape=(
            jax.ShapeDtypeStruct((IMG,), jnp.int32),
            jax.ShapeDtypeStruct((2 * NDP,), jnp.int32),
            jax.ShapeDtypeStruct((NDP, 8, 128), jnp.int32),
        ),
        in_specs=[SM],
        out_specs=(SM, SM, VM),
        scratch_shapes=[pltpu.SMEM((NDP,), jnp.int32)],
        compiler_params=params(),
    )(destination)


def dot_nn(a, b):
    return lax.dot_general(a, b, (((1,), (0,)), ((), ())), preferred_element_type=F32)


def dot_nt(a, b):
    return lax.dot_general(a, b, (((1,), (1,)), ((), ())), preferred_element_type=F32)


def window(h):
    low = (HD * h // 128) * 128
    high = -(-(HD * h + HD) // 128) * 128
    return low, high - low


PARTS = ((0, 4), (4, 4), (8, 4), (12, 3))
ORDER = (4, 3, -3, 2, -2, 1, -1, 0)


def block_kernel(
    lane_ref, inverse_ref, x_ref, w_ref, small_ref, count_ref, live_ref, cnt_ref, grad_ref,
    dx_ref, fin_ref, arr_ref, counts_ref,
    wf, small_all, cbuf, stage, garr, cvec, csm, starts,
    normed, normed_t, qkv, dqkv, g, att, probs, dn, inv, row, dgain,
    lanes, p_all, pair, ring_in, ring_out, total, plane, sums, sums_all,
    c_send, c_recv, g_send, g_recv, s_send, s_recv, w_send, w_recv, b_send, b_recv, l_sem,
    a_send, a_recv, p_send, p_recv, r_send, r_recv, x_send, x_recv, y_send, y_recv, f_send, f_recv, z_send, z_recv,
):
    me = lax.axis_index("dp")
    z = lax.axis_index("fsdp")
    core = lax.rem(me, 2)
    chip = me // 2
    sib = me + 1 - 2 * core
    ahead, behind = lax.rem(z + 1, NZ), lax.rem(z + NZ - 1, NZ)

    barrier = pltpu.get_barrier_semaphore()

    def greet(k, _):
        pl.semaphore_signal(barrier, inc=1, device_id={"dp": lax.rem(me + k, NDP)}, device_id_type=MESH)
        return 0

    lax.fori_loop(1, NDP, greet, 0)
    for k in range(1, NZ):
        pl.semaphore_signal(barrier, inc=1, device_id={"fsdp": lax.rem(z + k, NZ)}, device_id_type=MESH)
    wf[pl.ds(pl.multiple_of(z * SHARD, 16), SHARD), :] = w_ref[...]
    cbuf[me] = cnt_ref[me]
    small_all[z] = small_ref[...]
    pl.semaphore_wait(barrier, NDP - 1 + NZ - 1)

    def count_copy(k, slot):
        peer = lax.rem(me + k, NDP)
        return remote(cnt_ref.at[peer], cbuf.at[slot], c_send.at[k], c_recv.at[slot], {"dp": peer})

    def count_start(k, _):
        count_copy(k, me).start()
        return 0

    lax.fori_loop(1, NDP, count_start, 0)

    def rows_of(t):
        return pl.ds(pl.multiple_of(t * SHARD + core * HALF, 16), HALF)

    def gather_valid(d, s, q):
        return s < 3 or (s == 3 and (q < 2) == (d == 0))

    def gather_copy(d, s, q):
        t = lax.rem(z - s + NZ, NZ) if d == 0 else lax.rem(z + s, NZ)
        block = wf.at[rows_of(t), pl.ds(*COLS[q])]
        return remote(block, block, w_send.at[d, s, q], w_recv.at[d, s, q], {"fsdp": behind if d else ahead})

    def sib_copy(d, s, q):
        t = lax.rem(z - 1 - s + NZ, NZ) if d == 0 else lax.rem(z + 1 + s, NZ)
        block = wf.at[rows_of(t), pl.ds(*COLS[q])]
        return remote(block, block, b_send.at[d, s, q], b_recv.at[d, s, q], {"dp": sib})

    def small_copy(k, slot):
        return remote(
            small_ref, small_all.at[slot], s_send.at[k], s_recv.at[slot], {"fsdp": lax.rem(z + k, NZ)}
        )

    for k in range(1, NZ):
        small_copy(k, z).start()
    for q in range(4):
        for d in range(2):
            gather_copy(d, 0, q).start()

    def count_wait(k, _):
        count_copy(k, lax.rem(me + k, NDP)).wait()
        return 0

    lax.fori_loop(1, NDP, count_wait, 0)
    lane = lax.broadcasted_iota(jnp.int32, (8, 128), 1)
    tally = jnp.zeros((8, 128), jnp.int32)
    for s in range(NDP):
        tally = tally + jnp.where(lane == s, cbuf[s], 0)
    cvec[...] = tally
    counts_ref[...] = tally
    to_smem = pltpu.make_async_copy(cvec, csm, l_sem)
    to_smem.start()
    to_smem.wait()

    def prefix(s, start):
        starts[s] = start
        return start + csm[0, s]

    lax.fori_loop(0, NDP, prefix, jnp.int32(0))

    def grad_copy(k, slot):
        peer = lax.rem(me + k, NDP)
        return remote(stage.at[peer], garr.at[slot], g_send.at[k], g_recv.at[slot], {"dp": peer})

    def pick_grad(peer):
        first = jnp.minimum(starts[peer], RECV - 1)
        return grad_ref[first], grad_ref[jnp.minimum(first + 1, RECV - 1)]

    def grad_start(k, _):
        peer = lax.rem(me + k, NDP)
        stage[peer, 0], stage[peer, 1] = pick_grad(peer)
        grad_copy(k, me).start()
        return 0

    lax.fori_loop(1, NDP, grad_start, 0)
    garr[me, 0], garr[me, 1] = pick_grad(me)

    for k in range(1, NZ):
        small_copy(k, lax.rem(z + k, NZ)).wait()
    got = jnp.zeros((32, 128), F32)
    for s in range(NZ):
        got = got + small_all[s].astype(F32)
    for i in range(15):
        row[0:1, 128 * i : 128 * i + 128] = got[i : i + 1, :]
    for i in range(10):
        row[1:2, 128 * i : 128 * i + 128] = got[15 + i : 16 + i, :]

    def norm_block(b, _):
        rows = pl.ds(pl.multiple_of(b * 128, 128), 128)
        x = x_ref[rows, :].astype(F32)
        r = lax.rsqrt(jnp.mean(x * x, axis=-1, keepdims=True) + 1e-06)
        inv[rows, :] = jnp.broadcast_to(r, (128, 128))
        y = x * r * row[1:2, 0:D]
        normed[rows, :] = y.astype(BF)
        normed_t[:, rows] = y.T.astype(BF)
        return 0

    lax.fori_loop(0, 4, norm_block, 0)

    for s in range(4):
        for q in range(4):
            for d in range(2):
                if gather_valid(d, s, q):
                    gather_copy(d, s, q).wait_recv()
                    if gather_valid(d, s + 1, q):
                        gather_copy(d, s + 1, q).start()
                    sib_copy(d, s, q).start()
    for s in range(4):
        for q in range(4):
            for d in range(2):
                if gather_valid(d, s, q):
                    sib_copy(d, s, q).wait_recv()

    def project(n, _):
        cols = pl.ds(pl.multiple_of(n * 384, 128), 384)
        for m in range(2):
            r = dot_nn(normed[256 * m : 256 * m + 256, :], wf[:, cols]) + row[0:1, cols]
            qkv[256 * m : 256 * m + 256, cols] = r.astype(BF)
        return 0

    lax.fori_loop(0, 5, project, 0)

    dqkv[...] = jnp.zeros_like(dqkv)
    att[...] = jnp.zeros_like(att)
    scale = 1.0 / math.sqrt(HD)
    image = lax.broadcasted_iota(jnp.int32, (SLOT, 128), 1) // SLOT
    key = lax.broadcasted_iota(jnp.int32, (SLOT, 128), 0)

    def compact(t):
        acc = jnp.where(image == 0, t[0:SLOT], 0.0)
        for i in range(1, 8):
            acc = jnp.where(image == i, t[SLOT * i : SLOT * i + SLOT], acc)
        return acc

    def spread(t):
        return jnp.concatenate([jnp.where(image == i, t, 0.0) for i in range(8)], axis=0)

    def own(h, t):
        low, width = window(h)
        col = lax.broadcasted_iota(jnp.int32, (128, width), 1) + low
        return jnp.where((col >= HD * h) & (col < HD * h + HD), t, jnp.zeros((128, width), BF))

    def head_cols(h, part):
        low, width = window(h)
        return slice(part * W3 + low, part * W3 + low + width)

    def live_rows(b):
        return jnp.broadcast_to(live_ref[pl.ds(b, 1), :], (128, 128)).T[:, :1] > 0.5

    def attend(b, _):
        rows = pl.ds(pl.multiple_of(b * 128, 128), 128)
        keys = key < jnp.maximum(jnp.broadcast_to(count_ref[pl.ds(b, 1), :], (SLOT, 128)), 1)
        live = live_rows(b)
        for h in range(HEADS):
            q = own(h, qkv[rows, head_cols(h, 0)])
            s = jnp.where(keys, compact(dot_nt(qkv[rows, head_cols(h, 1)], q)) * scale, -1e30)
            e = jnp.exp(s - jnp.max(s, axis=0, keepdims=True))
            probs[b, h] = e / jnp.sum(e, axis=0, keepdims=True)
        for h in range(HEADS):
            v = own(h, qkv[rows, head_cols(h, 2)])
            o = jnp.where(live, dot_nn(spread(probs[b, h]).T.astype(BF), v), 0.0)
            at = pl.ds(pl.multiple_of(8 * b, 8), 8), slice(None), head_cols(h, 0)
            att[at] += o.astype(BF).reshape(8, SLOT, -1)
        return 0

    lax.fori_loop(0, 4, attend, 0)

    def att_copy(k, slot):
        peer = lax.rem(me + k, NDP)
        return remote(lanes.at[peer], arr_ref.at[slot], a_send.at[k], a_recv.at[slot], {"dp": peer})

    def att_start(k, _):
        peer = lax.rem(me + k, NDP)
        lanes[peer, 0] = att[inverse_ref[2 * peer]]
        lanes[peer, 1] = att[inverse_ref[2 * peer + 1]]
        att_copy(k, me).start()
        return 0

    lax.fori_loop(1, NDP, att_start, 0)
    arr_ref[me, 0] = att[inverse_ref[2 * me]]
    arr_ref[me, 1] = att[inverse_ref[2 * me + 1]]

    def grad_wait(k, _):
        grad_copy(k, lax.rem(me + k, NDP)).wait()
        return 0

    lax.fori_loop(1, NDP, grad_wait, 0)

    def take_grad(i, _):
        n = lane_ref[i]
        g[i] = garr[n // 2, lax.rem(n, 2)]
        return 0

    lax.fori_loop(0, IMG, take_grad, 0)

    def attend_back(b, _):
        rows = pl.ds(pl.multiple_of(b * 128, 128), 128)
        live = live_rows(b)
        for h in range(HEADS):
            low, width = window(h)
            q, k, v = (own(h, qkv[rows, head_cols(h, i)]) for i in range(3))
            gh = g[pl.ds(pl.multiple_of(8 * b, 8), 8), :, low : low + width].reshape(128, width)
            gh = jnp.where(live, own(h, gh), jnp.zeros((128, width), BF))
            p = probs[b, h]
            dp = compact(dot_nt(v, gh))
            ds = spread(p * (dp - jnp.sum(dp * p, axis=0, keepdims=True)) * scale)
            dq = dot_nn(ds.T.astype(BF), k)
            dk = dot_nn(ds.astype(BF), q)
            dv = dot_nn(spread(p).astype(BF), gh)
            dqkv[rows, head_cols(h, 0)] += dq.astype(BF)
            dqkv[rows, head_cols(h, 1)] += dk.astype(BF)
            dqkv[rows, head_cols(h, 2)] += dv.astype(BF)
        return 0

    lax.fori_loop(0, 4, attend_back, 0)

    def target(off):
        return lax.rem(z + off + NZ, NZ)

    def pair_copy(off):
        t = target(off)
        return remote(p_all.at[2 * t + 1 - core], pair.at[t], p_send.at[off + 3], p_recv.at[off + 3], {"dp": sib})

    def weight_grad(off):
        t = target(off)
        left = normed_t[pl.ds(pl.multiple_of(t * SHARD, 32), SHARD), :]
        for k in range(3):
            r = dot_nn(left, dqkv[:, 640 * k : 640 * k + 640]).astype(BF)
            p_all[pl.ds(2 * t, 2), 5 * k : 5 * k + 5] = r.reshape(2, 5, SLOT, 640)
        pair_copy(off).start()

    def ring_valid(d, s, q):
        return s > 0 or (q < 2) == (d == 0)

    def ring_copy(d, s, q):
        part = pl.ds(*PARTS[q])
        return remote(
            ring_out.at[d, s, part], ring_in.at[d, s, part], r_send.at[d, s, q], r_recv.at[d, s, q],
            {"fsdp": behind if d else ahead},
        )

    def mine(off, q):
        t = target(off)
        part = pl.ds(*PARTS[q])
        return p_all[2 * t + core, part].astype(F32) + pair[t, part].astype(F32)

    def ring_step(d, s, q):
        if not ring_valid(d, s, q):
            return
        part = pl.ds(*PARTS[q])
        r = mine(4 if s == 0 else (s - 4 if d else 4 - s), q)
        if s > 0 and ring_valid(d, s - 1, q):
            ring_copy(d, s - 1, q).wait_recv()
            r = r + ring_in[d, s - 1, part].astype(F32)
        ring_out[d, s, part] = r.astype(BF)
        ring_copy(d, s, q).start()

    def input_grad(n):
        cols = slice(256 * n, 256 * n + 256)
        for m in range(2):
            dn[256 * m : 256 * m + 256, cols] = dot_nt(dqkv[256 * m : 256 * m + 256, :], wf[cols, :])

    def finish(b, _):
        rows = pl.ds(pl.multiple_of(b * 32, 32), 32)
        x = x_ref[rows, :].astype(F32)
        r = inv[rows, 0:1]
        d = dn[rows, :]
        scaled = d * row[1:2, 0:D]
        m = jnp.mean(scaled * x, axis=-1, keepdims=True)
        dx_ref[rows, :] = (r * scaled - x * (r * r * r) * m).astype(BF)
        t = d * x * r
        dgain[...] += t[0:8] + t[8:16] + t[16:24] + t[24:32]
        return 0

    def bias_sum(b, acc):
        t = dqkv[pl.ds(pl.multiple_of(b * 32, 32), 32), :].astype(F32)
        return acc + (t[0:8] + t[8:16] + t[16:24] + t[24:32])

    def sums_copy(k, slot):
        return remote(sums, sums_all.at[slot], z_send.at[k], z_recv.at[slot], {"fsdp": lax.rem(z + k, NZ)})

    def small_sums():
        db = jnp.sum(lax.fori_loop(0, 16, bias_sum, jnp.zeros((8, QKV), F32)), axis=0, keepdims=True)
        dg = jnp.sum(dgain[...], axis=0, keepdims=True)
        out = [db[:, 128 * i : 128 * i + 128] for i in range(15)] + [dg[:, 128 * i : 128 * i + 128] for i in range(10)]
        out = jnp.concatenate(out + [jnp.zeros((7, 128), F32)], axis=0)
        sums[...] = out.astype(BF)
        sums_all[z] = out.astype(BF)
        for k in range(1, NZ):
            sums_copy(k, z).start()

    weight_grad(4)
    weight_grad(3)
    weight_grad(-3)
    pair_copy(4).wait_recv()
    for q in range(4):
        for d in range(2):
            ring_step(d, 0, q)
    for off in ORDER[3:]:
        weight_grad(off)
    dgain[...] = jnp.zeros_like(dgain)
    beside = [functools.partial(input_grad, n) for n in range(5)]
    beside += [lambda n=n: lax.fori_loop(4 * n, 4 * n + 4, finish, 0) for n in range(4)] + [small_sums]
    for s in range(1, 4):
        for d in range(2):
            pair_copy(s - 4 if d else 4 - s).wait_recv()
        for q in range(4):
            for d in range(2):
                ring_step(d, s, q)
            if beside:
                beside.pop(0)()
    pair_copy(0).wait_recv()
    for q in range(4):
        part = pl.ds(*PARTS[q])
        r = mine(0, q)
        for d in range(2):
            ring_copy(d, 3, q).wait_recv()
            r = r + ring_in[d, 3, part].astype(F32)
        total[part] = r.astype(BF)
    for k in range(1, NZ):
        sums_copy(k, lax.rem(z + k, NZ)).wait()
    r = jnp.zeros((32, 128), F32)
    for s in range(NZ):
        r = r + sums_all[s].astype(F32)
    r = [jnp.concatenate([r[5 * i + j : 5 * i + j + 1, :] for j in range(5)], axis=1) for i in range(5)]
    total[PIECES - 1] = jnp.concatenate(r + [jnp.zeros((11, 640), F32)], axis=0).astype(BF)

    def scatter_copy(k):
        i = lax.rem(chip + k, CHIPS)
        return remote(total.at[i], plane.at[chip], x_send.at[k], x_recv.at[chip], {"dp": 2 * i + core})

    def scatter_start(k, _):
        scatter_copy(k).start()
        return 0

    lax.fori_loop(1, CHIPS, scatter_start, 0)
    plane[chip] = total[chip]

    def scatter_wait(k, _):
        i = lax.rem(chip + k, CHIPS)
        remote(total.at[i], plane.at[i], x_send.at[k], x_recv.at[i], {"dp": 2 * i + core}).wait()
        return 0

    lax.fori_loop(1, CHIPS, scatter_wait, 0)
    r = jnp.zeros((SLOT, 640), F32)
    for i in range(CHIPS):
        r = r + plane[i].astype(F32)
    fin_ref[core, chip] = r.astype(BF)

    def share_copy(k, slot):
        i = lax.rem(chip + k, CHIPS)
        return remote(
            fin_ref.at[core, slot], fin_ref.at[core, slot], y_send.at[k], y_recv.at[slot], {"dp": 2 * i + core}
        )

    def share_start(k, _):
        share_copy(k, chip).start()
        return 0

    lax.fori_loop(1, CHIPS, share_start, 0)

    def share_wait(k, _):
        i = lax.rem(chip + k, CHIPS)
        share_copy(k, i).wait_recv()
        return 0

    lax.fori_loop(1, CHIPS, share_wait, 0)
    last = remote(fin_ref.at[core], fin_ref.at[core], f_send, f_recv, {"dp": sib})
    last.start()

    def share_sent(k, _):
        share_copy(k, chip).wait_send()
        return 0

    lax.fori_loop(1, CHIPS, share_sent, 0)
    for off in ORDER:
        pair_copy(off).wait_send()
    for s in range(4):
        for q in range(4):
            for d in range(2):
                if ring_valid(d, s, q):
                    ring_copy(d, s, q).wait_send()
                if gather_valid(d, s, q):
                    gather_copy(d, s, q).wait_send()
                    sib_copy(d, s, q).wait_send()

    def att_wait(k, _):
        att_copy(k, lax.rem(me + k, NDP)).wait()
        return 0

    lax.fori_loop(1, NDP, att_wait, 0)
    last.wait()


def block(lane, inverse, x, weight, small, count, live, cnt, grad):
    dma = pltpu.SemaphoreType.DMA
    vmem = pltpu.VMEM
    return pl.pallas_call(
        block_kernel,
        out_shape=(
            jax.ShapeDtypeStruct((ROWS, D), BF),
            jax.ShapeDtypeStruct((2, PIECES, SLOT, 640), BF),
            jax.ShapeDtypeStruct((NDP, 2, SLOT, W3), BF),
            jax.ShapeDtypeStruct((8, 128), jnp.int32),
        ),
        in_specs=[SM] * 2 + [VM] * 7,
        out_specs=(VM,) * 4,
        scratch_shapes=[
            vmem((D, QKV), BF),
            vmem((NZ, 32, 128), BF),
            vmem((NDP, 8, 128), jnp.int32),
            vmem((NDP, 2, SLOT, W3), BF),
            vmem((NDP, 2, SLOT, W3), BF),
            vmem((8, 128), jnp.int32),
            pltpu.SMEM((8, 128), jnp.int32),
            pltpu.SMEM((NDP,), jnp.int32),
            vmem((ROWS, D), BF),
            vmem((D, ROWS), BF),
            vmem((ROWS, QKV), BF),
            vmem((ROWS, QKV), BF),
            vmem((IMG, SLOT, W3), BF),
            vmem((IMG, SLOT, W3), BF),
            vmem((4, HEADS, SLOT, 128), F32),
            vmem((ROWS, D), F32),
            vmem((ROWS, 128), F32),
            vmem((8, QKV), F32),
            vmem((8, D), F32),
            vmem((NDP, 2, SLOT, W3), BF),
            vmem((2 * NZ, PIECES - 1, SLOT, 640), BF),
            vmem((NZ, PIECES - 1, SLOT, 640), BF),
            vmem((2, 4, PIECES - 1, SLOT, 640), BF),
            vmem((2, 4, PIECES - 1, SLOT, 640), BF),
            vmem((PIECES, SLOT, 640), BF),
            vmem((CHIPS, SLOT, 640), BF),
            vmem((32, 128), BF),
            vmem((NZ, 32, 128), BF),
            dma((NDP,)), dma((NDP,)), dma((NDP,)), dma((NDP,)), dma((NZ,)), dma((NZ,)),
            dma((2, 4, 4)), dma((2, 4, 4)), dma((2, 4, 4)), dma((2, 4, 4)), dma,
            dma((NDP,)), dma((NDP,)), dma((NZ,)), dma((NZ,)), dma((2, 4, 4)), dma((2, 4, 4)),
            dma((CHIPS,)), dma((CHIPS,)), dma((CHIPS,)), dma((CHIPS,)), dma, dma, dma((NZ,)), dma((NZ,)),
        ],
        compiler_params=params(1),
    )(lane, inverse, x, weight, small, count, live, cnt, grad)


def finish_kernel(counts_ref, fin_ref, arr_ref, att_ref, gw_ref, small_ref):
    scale = 1.0 / math.sqrt(NDP * NZ * ROWS)
    att_ref[...] = jnp.zeros_like(att_ref)

    def place(src, start):
        n = counts_ref[0, src]
        for k in range(2):

            @pl.when(n > k)
            def _():
                att_ref[jnp.minimum(start + k, RECV - 1)] = arr_ref[2 * src + k]

        return start + n

    lax.fori_loop(0, NDP, place, jnp.int32(0))
    for c in range(2):
        for i in range(PIECES - 1):
            r0, c0 = HALF * c + SLOT * (i % 5), 640 * (i // 5)
            gw_ref[r0 : r0 + SLOT, c0 : c0 + 640] = fin_ref[c, i].astype(F32) * scale
    small_ref[...] = (fin_ref[0, PIECES - 1].astype(F32) + fin_ref[1, PIECES - 1].astype(F32)) * scale


def finish(counts, fin, arr):
    return pl.pallas_call(
        finish_kernel,
        out_shape=(
            jax.ShapeDtypeStruct((RECV, SLOT, W3), BF),
            jax.ShapeDtypeStruct((SHARD, QKV), F32),
            jax.ShapeDtypeStruct((SLOT, 640), F32),
        ),
        in_specs=[SM, VM, VM],
        out_specs=(VM,) * 3,
        compiler_params=params(),
    )(counts, fin, arr)


def local(patches, patch_count, destination, qkv_weight, qkv_bias, norm_gain, grad_out):
    z = lax.axis_index("fsdp")
    small = jnp.zeros((4096,), BF)
    small = lax.dynamic_update_slice(small, qkv_bias, (z * (QKV // NZ),))
    small = lax.dynamic_update_slice(small, norm_gain, (QKV + z * SHARD,)).reshape(32, 128)
    count = jnp.broadcast_to(patch_count[:, None], (IMG, SLOT)).reshape(4, 128)
    live = (jnp.arange(SLOT)[None, :] < patch_count[:, None]).astype(F32).reshape(4, 128)
    lane, inverse, cnt = tables(destination)
    dx, fin, arr, counts = block(
        lane, inverse, patches, qkv_weight, small, count, live, cnt, grad_out.reshape(RECV, SLOT, W3)
    )
    att, gw, sums = finish(counts, fin, arr.reshape(2 * NDP, SLOT, W3))
    gb = lax.dynamic_slice(sums[0:3].reshape(QKV), (z * (QKV // NZ),), (QKV // NZ,))
    gg = lax.dynamic_slice(sums[3:5].reshape(D), (z * SHARD,), (SHARD,))
    return att.reshape(RECV * SLOT, W3), dx, gw, gb, gg


def solution(mesh):
    return jax.shard_map(
        local,
        mesh=mesh,
        in_specs=(
            P(("dp", "fsdp"), None),
            P(("dp", "fsdp")),
            P(("dp", "fsdp")),
            P("fsdp", None),
            P("fsdp"),
            P("fsdp"),
            P(("dp", "fsdp"), None),
        ),
        out_specs=(
            P(("dp", "fsdp"), None),
            P(("dp", "fsdp"), None),
            P("fsdp", None),
            P("fsdp"),
            P("fsdp"),
        ),
        check_vma=False,
    )
```

time: 152 us -> 124 us (0.82)
  Pallas kernels: 145 us -> 116 us
  local copies, waits for them, and re-layouts: 4.77 us -> 6.49 us
    pallas_call x3 -> x1, Pallas kernels: 139 us -> 110 us  [block(): pl.pallas_call(block_kernel, out_shape=(jax.ShapeDtypeStruct((ROWS, D), B...]
where the time goes in v2:
time: 124 us
  Pallas kernels  116 us (94%)
  local copies, waits for them, and re-layouts  6.49 us (5%)
    pallas_call x1, Pallas kernels, block(): pl.pallas_call(block_kernel, out_shape=(jax.ShapeDtypeStruct((ROWS, D), B...  110 us
    pallas_call x1, Pallas kernels, finish(): pl.pallas_call(finish_kernel, out_shape=(jax.ShapeDtypeStruct((RECV, SLOT...  3.78 us
    pallas_call x1, Pallas kernels, tables(): pl.pallas_call(table_kernel, out_shape=(jax.ShapeDtypeStruct((IMG,), jnp....  2.6 us

profile of v2, /device:TPU:1, one launch (start us, length us, event | category | flops | bytes accessed | tf_op | source)
XLA Modules:
  0.0 124.0 jit_solution(11603584031598003967)
XLA Ops:
  0.6 0.7 broadcast_in_dim.16
  1.4 0.1 lt.29
  1.5 0.9 dynamic_update_slice.6
  2.3 0.8 dynamic_update_slice.7
  3.2 0.0 copy-start.1
  3.2 0.1 broadcast_in_dim.17
  3.2 0.1 broadcast_in_dim.18.count_ref
  3.3 0.0 copy-start.2
  3.3 0.6 compare_convert_fusion.live_ref
  3.9 2.6 %shard_map.110 = (s32[32]{0:T(128)}, s32[64]{0:T(128)}, s32[32,8,128]{2,1,0:T(8,128)}) custom-call(s32[32]{0:T(128)} %dest_ref.1), custom_call_target="tpu_custom_call" | custom-call | tf_op jit(solution)/shard_map/pallas_call | solution.py:78
  6.5 0.0 copy-done.1
  6.5 0.0 copy-done.2
  6.5 109.8 %shard_map.111 = (bf16[512,1280]{1,0:T(8,128)(2,1)}, bf16[2,16,16,640]{3,2,1,0:T(8,128)(2,1)}, bf16[32,2,16,640]{3,2,1,0:T(8,128)(2,1)}, s32[8,128]{1,0:T(8,128)}) custom-call(s32[32]{0:T(128)} %get-tuple-element.15.lane_ref, s32[64]{0:T(128)} %get-tuple-element.16.inverse_ref, bf16[512,1280]{1,0:T(8,128)(2,1)} %x_ref.1, bf16[160,1920]{1,0:T(8,128)(2,1)} %w_ref.1, ...), custom_call_target="tpu_custom_call" | custom-call | tf_op jit(solution)/shard_map/pallas_call | solution.py:535
  116.4 0.0 copy-start
  116.4 3.8 %shard_map.112 = (bf16[56,16,640]{2,1,0:T(8,128)(2,1)}, f32[160,1920]{1,0:T(8,128)}, f32[16,640]{1,0:T(8,128)}) custom-call(s32[8,128]{1,0:T(8,128)} %get-tuple-element.18.counts_ref, bf16[2,16,16,640]{3,2,1,0:T(8,128)(2,1)} %get-tuple-element.19.fin_ref, bf16[64,16,640]{2,1,0:T(8,128)(2,1)} %bitcast.4), custom_call_target="tpu_custom_call" | custom-call | tf_op jit(solution)/shard_map/pallas_call | solution.py:606
  120.2 0.7 slice.7
  120.9 0.7 slice.6
  121.6 0.6 dynamic_slice.6
  122.3 0.6 dynamic_slice.7
  122.9 0.0 copy-done
  122.9 1.1 copy.15
  (4 shorter events, 0.0 us)
Async XLA Ops:
  3.2 3.3 %copy-start.1 = (bf16[4096]{0:T(1024)(128)(2,1)}, bf16[4096]{0:T(1024)(128)(2,1)S(1)}, u32[]{:S(2)}) copy-start(bf16[4096]{0:T(1024)(128)(2,1)S(1)} %dynamic_update_slice.7) | copy-start | bytes 24580
  3.3 3.2 %copy-start.2 = (s32[4,128]{1,0:T(4,128)}, s32[4,128]{1,0:T(4,128)S(1)}, u32[]{:S(2)}) copy-start(s32[4,128]{1,0:T(4,128)S(1)} %broadcast_in_dim.18.count_ref) | copy-start | bytes 6148
  116.4 6.6 %copy-start = (bf16[512,1280]{1,0:T(8,128)(2,1)S(1)}, bf16[512,1280]{1,0:T(8,128)(2,1)}, u32[]{:S(2)}) copy-start(bf16[512,1280]{1,0:T(8,128)(2,1)} %get-tuple-element.31) | copy-start | bytes 3932164

commit v3 on v2

v3 whole, which is shorter than its diff:
```python
import functools
import math

import jax
import jax.numpy as jnp
from jax import lax
from jax.experimental import pallas as pl
from jax.experimental.pallas import tpu as pltpu
from jax.sharding import PartitionSpec as P

MESH = pl.DeviceIdType.MESH
BF = jnp.bfloat16
F32 = jnp.float32
D = 1280
QKV = 1920
HEADS = 8
HD = 80
W3 = HEADS * HD
SLOT = 16
IMG = 32
ROWS = IMG * SLOT
RECV = 56
NDP = 32
NZ = 8
CHIPS = 16
SHARD = D // NZ
HALF = SHARD // 2
PIECES = 16
LIMIT = 58 * 2**20
GET = ((0, 384), (640, 384), (1280, 384), (384, 256), (1024, 256), (1664, 256))
PUT = ((0, 256), (640, 256), (1280, 256), (256, 384), (896, 384), (1536, 384))
ORDER = (4, 3, -3, 2, -2, 1, -1, 0)
VM = pl.BlockSpec(memory_space=pltpu.VMEM)
SM = pl.BlockSpec(memory_space=pltpu.SMEM)
ANY = pl.BlockSpec(memory_space=pl.ANY)


def remote(src, dst, send, recv, where):
    return pltpu.make_async_remote_copy(
        src_ref=src, dst_ref=dst, send_sem=send, recv_sem=recv, device_id=where, device_id_type=MESH
    )


def dot_nn(a, b):
    return lax.dot_general(a, b, (((1,), (0,)), ((), ())), preferred_element_type=F32)


def dot_nt(a, b):
    return lax.dot_general(a, b, (((1,), (1,)), ((), ())), preferred_element_type=F32)


def window(h):
    low = (HD * h // 128) * 128
    high = -(-(HD * h + HD) // 128) * 128
    return low, high - low


def block_kernel(
    dest_ref, amount_ref, small_ref, x_hbm, w_hbm, grad_hbm,
    dx_hbm, att_hbm, gw_hbm, gb_ref, gg_ref,
    x_ref, grad_ref, dx_ref, out_ref, gw_ref,
    wf, small_all, cmine, cbuf, stage, garr, tabs, csm, lane_sm, inverse_sm, slot_sm, starts,
    normed, normed_t, qkv, dqkv, g, att, probs, dn, inv, row, dgain, count_v, live_v,
    lanes, arr, p_all, pair, ring_in, ring_out, tot, tot_small, plane0, plane1, fin0, fin1, sums, sums_all,
    l_sem, c_sem, g_sem, s_sem, a_sem, z_sem, x_sem, y_sem, f_sem, w_send, w_recv, b_send, b_recv,
    p_send, p_recv, r_send, r_recv,
):
    me = lax.axis_index("dp")
    z = lax.axis_index("fsdp")
    core = lax.rem(me, 2)
    chip = me // 2
    sib = me + 1 - 2 * core
    ahead, behind = lax.rem(z + 1, NZ), lax.rem(z + NZ - 1, NZ)
    plane, fin = (plane0, plane1), (fin0, fin1)

    def many(like, sems):
        return remote(like, like, sems.at[0], sems.at[1], {"dp": sib})

    x_in = pltpu.make_async_copy(x_hbm, x_ref, l_sem.at[0])
    w_in = pltpu.make_async_copy(w_hbm, wf.at[pl.ds(pl.multiple_of(z * SHARD, 32), SHARD), :], l_sem.at[1])
    grad_in = pltpu.make_async_copy(grad_hbm, grad_ref, l_sem.at[2])
    w_in.start()
    grad_in.start()
    x_in.start()

    barrier = pltpu.get_barrier_semaphore()

    def greet(k, _):
        pl.semaphore_signal(barrier, inc=1, device_id={"dp": lax.rem(me + k, NDP)}, device_id_type=MESH)
        return 0

    lax.fori_loop(1, NDP, greet, 0)
    for k in range(1, NZ):
        pl.semaphore_signal(barrier, inc=1, device_id={"fsdp": lax.rem(z + k, NZ)}, device_id_type=MESH)

    lane = lax.broadcasted_iota(jnp.int32, (1, 128), 1)
    dests = [dest_ref[i] for i in range(IMG)]
    per = jnp.zeros((1, 128), jnp.int32)
    to = jnp.zeros((1, 128), jnp.int32)
    for i in range(IMG):
        per = per + jnp.where(lane == dests[i], 1, 0)
        to = jnp.where(lane == i, dests[i], to)
    cmine[0] = per
    cbuf[me] = per
    rank = jnp.zeros((1, 128), jnp.int32)
    for i in range(IMG):
        rank = rank + jnp.where((to == dests[i]) & (lane > i), 1, 0)
    tabs[0] = 2 * to + jnp.minimum(rank, 1)
    lane_copy = pltpu.make_async_copy(tabs.at[pl.ds(0, 1)], lane_sm, l_sem.at[3])
    lane_copy.start()
    lane_copy.wait()
    source = jnp.zeros((1, 128), jnp.int32)
    for i in range(IMG):
        source = jnp.where(lane == lane_sm[0, 0, i], i, source)
    tabs[1] = source
    inverse_copy = pltpu.make_async_copy(tabs.at[pl.ds(1, 1)], inverse_sm, l_sem.at[4])
    inverse_copy.start()
    for b in range(4):
        have = jnp.zeros((1, 128), jnp.int32)
        for i in range(8):
            have = jnp.where(lane // SLOT == i, amount_ref[8 * b + i], have)
        count_v[b : b + 1, :] = have
        live_v[b : b + 1, :] = jnp.where(lax.rem(lane, SLOT) < have, 1.0, 0.0)
    small_all[z] = small_ref[...]
    w_in.wait()
    pl.semaphore_wait(barrier, NDP - 1 + NZ - 1)

    def rows_of(t):
        return pl.ds(pl.multiple_of(t * SHARD + core * HALF, 16), HALF)

    def gather_valid(d, s, q):
        return s < 3 or (s == 3 and (q in (0, 1, 3)) == (d == 0))

    def got_shard(d, s):
        return lax.rem(z - 1 - s + NZ, NZ) if d == 0 else lax.rem(z + 1 + s, NZ)

    def gather_copy(d, s, q):
        block = wf.at[rows_of(got_shard(d, s - 1)), pl.ds(*GET[q])]
        return remote(block, block, w_send, w_recv.at[d, s, q], {"fsdp": behind if d else ahead})

    def gather_start(h):
        for q in range(3 * h, 3 * h + 3):
            for d in range(2):
                gather_copy(d, 0, q).start()

    def gather_step(h, s):
        for q in range(3 * h, 3 * h + 3):
            for d in range(2):
                if not gather_valid(d, s, q):
                    continue
                gather_copy(d, s, q).wait_recv()
                if gather_valid(d, s + 1, q):
                    gather_copy(d, s + 1, q).start()
                block = wf.at[rows_of(got_shard(d, s)), pl.ds(*GET[q])]
                remote(block, block, b_send, b_recv.at[h], {"dp": sib}).start()

    def gather_end(h):
        like = wf.at[pl.ds(0, 7 * HALF), pl.ds(0, 768 if h else 1152)]
        remote(like, like, b_send, b_recv.at[h], {"dp": sib}).wait_recv()

    def count_start(k, _):
        remote(cmine.at[0], cbuf.at[me], c_sem.at[0], c_sem.at[1], {"dp": lax.rem(me + k, NDP)}).start()
        return 0

    gather_start(0)
    lax.fori_loop(1, NDP, count_start, 0)

    for k in range(1, NZ):
        remote(small_ref, small_all.at[z], s_sem.at[0], s_sem.at[1], {"fsdp": lax.rem(z + k, NZ)}).start()

    many(cbuf.at[pl.ds(0, NDP - 1)], c_sem).wait()
    to_smem = pltpu.make_async_copy(cbuf, csm, l_sem.at[3])
    to_smem.start()
    to_smem.wait()

    def prefix(s, carry):
        start, table = carry
        n = csm[s, 0, me]
        starts[s] = start
        table = jnp.where((lane >= start) & (lane < start + n), 2 * s + lane - start, table)
        return start + n, table

    _, table = lax.fori_loop(0, NDP, prefix, (jnp.int32(0), jnp.full((1, 128), -1, jnp.int32)))
    tabs[2] = table
    inverse_copy.wait()
    slot_copy = pltpu.make_async_copy(tabs.at[pl.ds(2, 1)], slot_sm, l_sem.at[4])
    slot_copy.start()

    def pick_grad(peer):
        first = jnp.minimum(starts[peer], RECV - 1)
        return grad_ref[first], grad_ref[jnp.minimum(first + 1, RECV - 1)]

    def grad_start(k, _):
        peer = lax.rem(me + k, NDP)
        stage[peer, 0], stage[peer, 1] = pick_grad(peer)
        remote(stage.at[peer], garr.at[me], g_sem.at[0], g_sem.at[1], {"dp": peer}).start()
        return 0

    grad_in.wait()
    gather_step(0, 0)
    lax.fori_loop(1, 16, grad_start, 0)
    gather_step(0, 1)
    lax.fori_loop(16, NDP, grad_start, 0)
    garr[me, 0], garr[me, 1] = pick_grad(me)

    many(small_all.at[pl.ds(0, NZ - 1)], s_sem).wait()
    for s in range(NZ):
        row[0:1, 240 * s : 240 * s + 240] = small_all[s, 0:1, 0:240]
        row[1:2, 160 * s : 160 * s + 160] = small_all[s, 1:2, 0:160]
    x_in.wait()

    def norm_block(b, _):
        rows = pl.ds(pl.multiple_of(b * 128, 128), 128)
        x = x_ref[rows, :].astype(F32)
        r = lax.rsqrt(jnp.mean(x * x, axis=-1, keepdims=True) + 1e-06)
        inv[rows, :] = jnp.broadcast_to(r, (128, 128))
        y = x * r * row[1:2, 0:D]
        normed[rows, :] = y.astype(BF)
        normed_t[:, rows] = y.T.astype(BF)
        return 0

    lax.fori_loop(0, 4, norm_block, 0)
    dqkv[...] = jnp.zeros_like(dqkv)
    att[...] = jnp.zeros_like(att)
    dgain[...] = jnp.zeros_like(dgain)

    def project(h):
        for low, width in GET[3 * h : 3 * h + 3]:
            for m in range(2):
                r = dot_nn(normed[256 * m : 256 * m + 256, :], wf[:, low : low + width]) + row[0:1, low : low + width]
                qkv[256 * m : 256 * m + 256, low : low + width] = r.astype(BF)

    scale = 1.0 / math.sqrt(HD)
    image = lax.broadcasted_iota(jnp.int32, (SLOT, 128), 1) // SLOT
    key = lax.broadcasted_iota(jnp.int32, (SLOT, 128), 0)

    def compact(t):
        acc = jnp.where(image == 0, t[0:SLOT], 0.0)
        for i in range(1, 8):
            acc = jnp.where(image == i, t[SLOT * i : SLOT * i + SLOT], acc)
        return acc

    def spread(t):
        return jnp.concatenate([jnp.where(image == i, t, 0.0) for i in range(8)], axis=0)

    def own(h, t):
        low, width = window(h)
        col = lax.broadcasted_iota(jnp.int32, (128, width), 1) + low
        return jnp.where((col >= HD * h) & (col < HD * h + HD), t, jnp.zeros((128, width), BF))

    def head_cols(h, part):
        low, width = window(h)
        return slice(part * W3 + low, part * W3 + low + width)

    def live_rows(b):
        return jnp.broadcast_to(live_v[pl.ds(b, 1), :], (128, 128)).T[:, :1] > 0.5

    def attend(heads, b, _):
        rows = pl.ds(pl.multiple_of(b * 128, 128), 128)
        keys = key < jnp.maximum(jnp.broadcast_to(count_v[pl.ds(b, 1), :], (SLOT, 128)), 1)
        live = live_rows(b)
        for h in heads:
            q = own(h, qkv[rows, head_cols(h, 0)])
            s = jnp.where(keys, compact(dot_nt(qkv[rows, head_cols(h, 1)], q)) * scale, -1e30)
            e = jnp.exp(s - jnp.max(s, axis=0, keepdims=True))
            probs[b, h] = e / jnp.sum(e, axis=0, keepdims=True)
        for h in heads:
            v = own(h, qkv[rows, head_cols(h, 2)])
            o = jnp.where(live, dot_nn(spread(probs[b, h]).T.astype(BF), v), 0.0)
            at = pl.ds(pl.multiple_of(8 * b, 8), 8), slice(None), head_cols(h, 0)
            att[at] += o.astype(BF).reshape(8, SLOT, -1)
        return 0

    def att_cols(h):
        return pl.ds(256, 384) if h else pl.ds(0, 256)

    def att_start(h, k, _):
        peer = lax.rem(me + k, NDP)
        cols = att_cols(h)
        for i in range(2):
            lanes[peer, i, :, cols] = att[inverse_sm[0, 0, 2 * peer + i], :, cols]
        src, dst = lanes.at[peer, :, :, cols], arr.at[me, :, :, cols]
        remote(src, dst, a_sem.at[h, 0], a_sem.at[h, 1], {"dp": peer}).start()
        return 0

    def att_send(h):
        lax.fori_loop(1, NDP, functools.partial(att_start, h), 0)
        cols = att_cols(h)
        for i in range(2):
            arr[me, i, :, cols] = att[inverse_sm[0, 0, 2 * me + i], :, cols]

    def take_grad(i, _):
        n = lane_sm[0, 0, i]
        g[i] = garr[n // 2, lax.rem(n, 2)]
        return 0

    def attend_back(heads, b, _):
        rows = pl.ds(pl.multiple_of(b * 128, 128), 128)
        live = live_rows(b)
        for h in heads:
            low, width = window(h)
            q, k, v = (own(h, qkv[rows, head_cols(h, i)]) for i in range(3))
            gh = g[pl.ds(pl.multiple_of(8 * b, 8), 8), :, low : low + width].reshape(128, width)
            gh = jnp.where(live, own(h, gh), jnp.zeros((128, width), BF))
            p = probs[b, h]
            dp = compact(dot_nt(v, gh))
            ds = spread(p * (dp - jnp.sum(dp * p, axis=0, keepdims=True)) * scale)
            dq = dot_nn(ds.T.astype(BF), k)
            dk = dot_nn(ds.astype(BF), q)
            dv = dot_nn(spread(p).astype(BF), gh)
            dqkv[rows, head_cols(h, 0)] += dq.astype(BF)
            dqkv[rows, head_cols(h, 1)] += dk.astype(BF)
            dqkv[rows, head_cols(h, 2)] += dv.astype(BF)
        return 0

    def target(off):
        return lax.rem(z + off + NZ, NZ)

    def weight_grad(h, *offs):
        for off in offs:
            t = target(off)
            left = normed_t[pl.ds(pl.multiple_of(t * SHARD, 32), SHARD), :]
            for low, width in PUT[3 * h : 3 * h + 3]:
                cols = pl.ds(low, width)
                p_all[t, :, :, cols] = dot_nn(left, dqkv[:, cols]).astype(BF).reshape(2, HALF, width)
                src, dst = p_all.at[t, 1 - core, :, cols], pair.at[t, :, cols]
                remote(src, dst, p_send, p_recv.at[h, off + 3], {"dp": sib}).start()

    def pair_wait(h, *offs):
        for off in offs:
            like = pair.at[target(off), :, pl.ds(0, 1152 if h else 768)]
            remote(like, like, p_send, p_recv.at[h, off + 3], {"dp": sib}).wait_recv()

    def ring_valid(d, s, q):
        return s > 0 or (q in (0, 1, 3)) == (d == 0)

    def ring_copy(d, s, q):
        cols = pl.ds(*PUT[q])
        return remote(
            ring_out.at[d, s, :, cols], ring_in.at[d, s, :, cols], r_send, r_recv.at[d, s, q],
            {"fsdp": behind if d else ahead},
        )

    def mine(off, q):
        t = target(off)
        cols = pl.ds(*PUT[q])
        return p_all[t, core, :, cols].astype(F32) + pair[t, :, cols].astype(F32)

    def ring_step(h, s):
        if s == 0:
            pair_wait(h, 4)
        else:
            pair_wait(h, 4 - s, s - 4)
        for q in range(3 * h, 3 * h + 3):
            for d in range(2):
                if not ring_valid(d, s, q):
                    continue
                cols = pl.ds(*PUT[q])
                r = mine(4 if s == 0 else (s - 4 if d else 4 - s), q)
                if s > 0 and ring_valid(d, s - 1, q):
                    ring_copy(d, s - 1, q).wait_recv()
                    r = r + ring_in[d, s - 1, :, cols].astype(F32)
                ring_out[d, s, :, cols] = r.astype(BF)
                ring_copy(d, s, q).start()

    def input_grad(n):
        cols = slice(256 * n, 256 * n + 256)
        for m in range(2):
            dn[256 * m : 256 * m + 256, cols] = dot_nt(dqkv[256 * m : 256 * m + 256, :], wf[cols, :])

    def finish(b, _):
        rows = pl.ds(pl.multiple_of(b * 32, 32), 32)
        x = x_ref[rows, :].astype(F32)
        r = inv[rows, 0:1]
        d = dn[rows, :]
        scaled = d * row[1:2, 0:D]
        m = jnp.mean(scaled * x, axis=-1, keepdims=True)
        dx_ref[rows, :] = (r * scaled - x * (r * r * r) * m).astype(BF)
        t = d * x * r
        dgain[...] += t[0:8] + t[8:16] + t[16:24] + t[24:32]
        return 0

    def bias_sum(b, acc):
        t = dqkv[pl.ds(pl.multiple_of(b * 32, 32), 32), :].astype(F32)
        return acc + (t[0:8] + t[8:16] + t[16:24] + t[24:32])

    dx_out = pltpu.make_async_copy(dx_ref, dx_hbm, l_sem.at[0])

    def small_sums():
        dx_out.start()
        db = jnp.sum(lax.fori_loop(0, 16, bias_sum, jnp.zeros((8, QKV), F32)), axis=0, keepdims=True)
        dg = jnp.sum(dgain[...], axis=0, keepdims=True)
        out = [db[:, 128 * i : 128 * i + 128] for i in range(15)] + [dg[:, 128 * i : 128 * i + 128] for i in range(10)]
        out = jnp.concatenate(out + [jnp.zeros((7, 128), F32)], axis=0)
        sums[...] = out.astype(BF)
        sums_all[z] = out.astype(BF)
        for k in range(1, NZ):
            remote(sums, sums_all.at[z], z_sem.at[0], z_sem.at[1], {"fsdp": lax.rem(z + k, NZ)}).start()

    def piece(h, i):
        return pl.ds(SLOT * (i % 5), SLOT), pl.ds(*PUT[3 * h + i // 5])

    def scatter(h, i):
        src = tot_small.at[:, pl.ds(0, 384 if h else 256)] if i == PIECES - 1 else tot.at[piece(h, i)]

        @pl.when(chip != i)
        def _():
            remote(src, plane[h].at[chip], x_sem.at[h, 0], x_sem.at[h, 1], {"dp": 2 * i + core}).start()

        @pl.when(chip == i)
        def _():
            plane[h][i] = src[...]

    def ring_end(h):
        pair_wait(h, 0)
        for q in range(3 * h, 3 * h + 3):
            cols = pl.ds(*PUT[q])
            r = mine(0, q)
            for d in range(2):
                ring_copy(d, 3, q).wait_recv()
                r = r + ring_in[d, 3, :, cols].astype(F32)
            tot[:, cols] = r.astype(BF)
            for i in range(5 * (q - 3 * h), 5 * (q - 3 * h) + 5):
                scatter(h, i)

    def plane_sum(h):
        many(plane[h].at[pl.ds(0, CHIPS - 1)], x_sem.at[h]).wait()
        r = plane[h][0].astype(F32)
        for i in range(1, CHIPS):
            r = r + plane[h][i].astype(F32)
        fin[h][core, chip] = r.astype(BF)
        block = fin[h].at[core, chip]

        def share_start(k, _):
            i = lax.rem(chip + k, CHIPS)
            remote(block, block, y_sem.at[h, 0], y_sem.at[h, 1], {"dp": 2 * i + core}).start()
            return 0

        lax.fori_loop(1, CHIPS, share_start, 0)

    def last_copy(h):
        return remote(fin[h].at[core], fin[h].at[core], f_sem.at[h, 0], f_sem.at[h, 1], {"dp": sib})

    def plane_end(h):
        many(fin[h].at[core, pl.ds(0, CHIPS - 1)], y_sem.at[h]).wait()
        last_copy(h).start()

    out_scale = 1.0 / math.sqrt(NDP * NZ * ROWS)

    def write_sums(h):
        last_copy(h).wait()
        for c in range(2):
            for i in range(PIECES - 1):
                rows, cols = piece(h, i)
                gw_ref[pl.ds(rows.start + HALF * c, SLOT), cols] = fin[h][c, i].astype(F32) * out_scale

    low_heads, high_heads = range(4), range(4, HEADS)
    gather_step(0, 2)
    gather_start(1)
    gather_step(0, 3)
    gather_end(0)
    project(0)
    gather_step(1, 0)
    lax.fori_loop(0, 4, functools.partial(attend, low_heads), 0)
    gather_step(1, 1)
    att_send(0)
    many(garr.at[pl.ds(0, NDP - 1)], g_sem).wait()
    lax.fori_loop(0, IMG, take_grad, 0)
    lax.fori_loop(0, 4, functools.partial(attend_back, low_heads), 0)
    gather_step(1, 2)
    weight_grad(0, 4, 3, -3)
    gather_step(1, 3)
    ring_step(0, 0)
    weight_grad(0, 2, -2, 1, -1, 0)
    gather_end(1)
    project(1)
    ring_step(0, 1)
    lax.fori_loop(0, 4, functools.partial(attend, high_heads), 0)
    ring_step(0, 2)
    lax.fori_loop(0, 4, functools.partial(attend_back, high_heads), 0)
    weight_grad(1, 4)
    ring_step(0, 3)
    weight_grad(1, 3, -3)
    ring_step(1, 0)
    att_send(1)
    weight_grad(1, 2, -2)
    ring_step(1, 1)
    weight_grad(1, 1, -1, 0)
    tot_small[...] = jnp.zeros_like(tot_small)
    scatter(0, PIECES - 1)
    ring_end(0)
    for n in range(3):
        input_grad(n)
    ring_step(1, 2)
    for n in range(3, 5):
        input_grad(n)
    lax.fori_loop(0, 8, finish, 0)
    ring_step(1, 3)
    lax.fori_loop(8, 16, finish, 0)
    small_sums()
    ring_end(1)
    plane_sum(0)
    many(sums_all.at[pl.ds(0, NZ - 1)], z_sem).wait()
    r = jnp.zeros((32, 128), F32)
    for s in range(NZ):
        r = r + sums_all[s].astype(F32)
    r = [jnp.concatenate([r[3 * i + j : 3 * i + j + 1, :] for j in range(3)], axis=1) for i in range(9)]
    tot_small[...] = jnp.concatenate(r + [jnp.zeros((7, 384), F32)], axis=0).astype(BF)
    scatter(1, PIECES - 1)

    for h in range(2):
        many(arr.at[pl.ds(0, NDP - 1), :, :, att_cols(h)], a_sem.at[h]).wait()
    slot_copy.wait()

    def place(i, _):
        n = slot_sm[0, 0, i]
        at = jnp.maximum(n, 0)
        block = arr[at // 2, lax.rem(at, 2)]
        out_ref[i] = jnp.where(n >= 0, block, jnp.zeros_like(block))
        return 0

    plane_sum(1)
    plane_end(0)
    lax.fori_loop(0, RECV, place, 0)
    att_out = pltpu.make_async_copy(out_ref, att_hbm, l_sem.at[1])
    att_out.start()
    write_sums(0)
    plane_end(1)
    write_sums(1)
    gw_out = pltpu.make_async_copy(gw_ref, gw_hbm, l_sem.at[2])
    gw_out.start()
    r = (fin1[0, PIECES - 1].astype(F32) + fin1[1, PIECES - 1].astype(F32)) * out_scale
    for i in range(25):
        part = r[i // 3 : i // 3 + 1, 128 * (i % 3) : 128 * (i % 3) + 128]
        if i < 15:
            row[2:3, 128 * i : 128 * i + 128] = part
        else:
            row[3:4, 128 * (i - 15) : 128 * (i - 15) + 128] = part
    gb = jnp.zeros((1, 240), F32)
    gg = jnp.zeros((1, 160), F32)
    for s in range(NZ):
        gb = jnp.where(z == s, row[2:3, 240 * s : 240 * s + 240], gb)
        gg = jnp.where(z == s, row[3:4, 160 * s : 160 * s + 160], gg)
    gb_ref[...] = gb
    gg_ref[...] = gg

    ring_like = wf.at[pl.ds(0, 560), :]
    pair_like = wf.at[pl.ds(0, 640), :]
    remote(ring_like, ring_like, w_send, w_recv.at[0, 0, 0], {"dp": sib}).wait_send()
    remote(ring_like, ring_like, b_send, b_recv.at[0], {"dp": sib}).wait_send()
    remote(ring_like, ring_like, r_send, r_recv.at[0, 0, 0], {"dp": sib}).wait_send()
    remote(pair_like, pair_like, p_send, p_recv.at[0, 0], {"dp": sib}).wait_send()
    dx_out.wait()
    att_out.wait()
    gw_out.wait()


def block(dest, amount, small, x, weight, grad):
    dma = pltpu.SemaphoreType.DMA
    vmem = pltpu.VMEM
    smem = pltpu.SMEM
    i32 = jnp.int32
    return pl.pallas_call(
        block_kernel,
        out_shape=(
            jax.ShapeDtypeStruct((ROWS, D), BF),
            jax.ShapeDtypeStruct((RECV, SLOT, W3), BF),
            jax.ShapeDtypeStruct((SHARD, QKV), F32),
            jax.ShapeDtypeStruct((1, 240), F32),
            jax.ShapeDtypeStruct((1, 160), F32),
        ),
        in_specs=[SM, SM, VM, ANY, ANY, ANY],
        out_specs=(ANY, ANY, ANY, VM, VM),
        scratch_shapes=[
            vmem((ROWS, D), BF),
            vmem((RECV, SLOT, W3), BF),
            vmem((ROWS, D), BF),
            vmem((RECV, SLOT, W3), BF),
            vmem((SHARD, QKV), F32),
            vmem((D, QKV), BF),
            vmem((NZ, 8, 256), F32),
            vmem((1, 1, 128), i32),
            vmem((NDP, 1, 128), i32),
            vmem((NDP, 2, SLOT, W3), BF),
            vmem((NDP, 2, SLOT, W3), BF),
            vmem((3, 1, 128), i32),
            smem((NDP, 1, 128), i32),
            smem((1, 1, 128), i32),
            smem((1, 1, 128), i32),
            smem((1, 1, 128), i32),
            smem((NDP,), i32),
            vmem((ROWS, D), BF),
            vmem((D, ROWS), BF),
            vmem((ROWS, QKV), BF),
            vmem((ROWS, QKV), BF),
            vmem((IMG, SLOT, W3), BF),
            vmem((IMG, SLOT, W3), BF),
            vmem((4, HEADS, SLOT, 128), F32),
            vmem((ROWS, D), F32),
            vmem((ROWS, 128), F32),
            vmem((8, QKV), F32),
            vmem((8, D), F32),
            vmem((8, 128), i32),
            vmem((8, 128), F32),
            vmem((NDP, 2, SLOT, W3), BF),
            vmem((NDP, 2, SLOT, W3), BF),
            vmem((NZ, 2, HALF, QKV), BF),
            vmem((NZ, HALF, QKV), BF),
            vmem((2, 4, HALF, QKV), BF),
            vmem((2, 4, HALF, QKV), BF),
            vmem((HALF, QKV), BF),
            vmem((SLOT, 384), BF),
            vmem((CHIPS, SLOT, 256), BF),
            vmem((CHIPS, SLOT, 384), BF),
            vmem((2, CHIPS, SLOT, 256), BF),
            vmem((2, CHIPS, SLOT, 384), BF),
            vmem((32, 128), BF),
            vmem((NZ, 32, 128), BF),
            dma((5,)),
            dma((2,)), dma((2,)), dma((2,)), dma((2, 2)), dma((2,)), dma((2, 2)), dma((2, 2)), dma((2, 2)),
            dma, dma((2, 4, 6)), dma, dma((2,)), dma, dma((2, 8)), dma, dma((2, 4, 6)),
        ],
        compiler_params=pltpu.CompilerParams(vmem_limit_bytes=LIMIT, collective_id=1, has_side_effects=True),
    )(dest, amount, small, x, weight, grad)


def hand_out_kernel(dx_in, att_in, gw_in, gb_in, gg_in, dx_out, att_out, gw_out, gb_out, gg_out, dx, att, gw, sems):
    steps = []
    for n, (src, mid, dst) in enumerate(((dx_in, dx, dx_out), (att_in, att, att_out), (gw_in, gw, gw_out))):
        size = src.shape[0] // 4
        for i in range(4):
            part = pl.ds(size * i, size)
            get = pltpu.make_async_copy(src.at[part], mid.at[part], sems.at[0, n, i])
            put = pltpu.make_async_copy(mid.at[part], dst.at[part], sems.at[1, n, i])
            get.start()
            steps.append((get, put))
    gb_out[...] = gb_in[...]
    gg_out[...] = gg_in[...]
    for get, put in steps:
        get.wait()
        put.start()
    for get, put in steps:
        put.wait()


def hand_out(*arrays):
    return pl.pallas_call(
        hand_out_kernel,
        out_shape=tuple(jax.ShapeDtypeStruct(a.shape, a.dtype) for a in arrays),
        in_specs=[ANY, ANY, ANY, VM, VM],
        out_specs=(ANY, ANY, ANY, VM, VM),
        scratch_shapes=[pltpu.VMEM(a.shape, a.dtype) for a in arrays[:3]] + [pltpu.SemaphoreType.DMA((2, 3, 4))],
        compiler_params=pltpu.CompilerParams(vmem_limit_bytes=LIMIT),
    )(*arrays)


def local(patches, patch_count, destination, qkv_weight, qkv_bias, norm_gain, grad_out):
    small = jnp.stack([jnp.pad(qkv_bias, (0, 16)), jnp.pad(norm_gain, (0, 96))]).astype(F32)
    small = jnp.pad(small, ((0, 6), (0, 0)))
    dx, att, gw, gb, gg = block(
        destination, patch_count, small, patches, qkv_weight, grad_out.reshape(RECV, SLOT, W3)
    )
    dx, att, gw, gb, gg = hand_out(dx, att, gw, gb, gg)
    return att.reshape(RECV * SLOT, W3), dx, gw, gb.reshape(-1), gg.reshape(-1)


def solution(mesh):
    return jax.shard_map(
        local,
        mesh=mesh,
        in_specs=(
            P(("dp", "fsdp"), None),
            P(("dp", "fsdp")),
            P(("dp", "fsdp")),
            P("fsdp", None),
            P("fsdp"),
            P("fsdp"),
            P(("dp", "fsdp"), None),
        ),
        out_specs=(
            P(("dp", "fsdp"), None),
            P(("dp", "fsdp"), None),
            P("fsdp", None),
            P("fsdp"),
            P("fsdp"),
        ),
        check_vma=False,
    )
```

time: 124 us -> 115 us (0.927)
  local copies, waits for them, and re-layouts: 6.49 us -> 1.33 us
  Pallas kernels: 116 us -> 112 us
    pallas_call x1, Pallas kernels: 110 us -> 107 us  [block(): pl.pallas_call(block_kernel, out_shape=(jax.ShapeDtypeStruct((ROWS, D), B...]
    pallas_call x2 -> x1, Pallas kernels: 6.38 us -> 4.44 us  [hand_out(): pl.pallas_call(hand_out_kernel, out_shape=tuple((jax.ShapeDtypeStruct(a.s...]
    dynamic_update_slice x2 -> x0, local copies, waits for them, and re-layouts: 1.69 us -> none  [the longest x1 0.86 us: local(): small = lax.dynamic_update_slice(small, qkv_bias, (z * (QKV // NZ),))]
    slice x2 -> x0, local copies, waits for them, and re-layouts: 1.46 us -> none  [the longest x1 0.73 us: local(): gg = lax.dynamic_slice(sums[3:5].reshape(D), (z * SHARD,), (SHARD,))]
    pad x0 -> x2, local copies, waits for them, and re-layouts: none -> 1.32 us  [the longest x1 0.66 us: local(): jnp.pad(qkv_bias, (0, 16))]
    dynamic_slice x2 -> x0, local copies, waits for them, and re-layouts: 1.27 us -> none  [the longest x1 0.64 us: local(): lax.dynamic_slice(sums[0:3].reshape(QKV), (z * (QKV // NZ),), (QKV // NZ,))]
where the time goes in v3:
time: 115 us; the launch traced here: 114 us
  Pallas kernels  112 us (97%)
  local copies, waits for them, and re-layouts  1.33 us (1%)
    pallas_call x1, Pallas kernels, block(): pl.pallas_call(block_kernel, out_shape=(jax.ShapeDtypeStruct((ROWS, D), B...  107 us
    pallas_call x1, Pallas kernels, hand_out(): pl.pallas_call(hand_out_kernel, out_shape=tuple((jax.ShapeDtypeStruct(a.s...  4.44 us

profile of v3, /device:TPU:1, one launch (start us, length us, event | category | flops | bytes accessed | tf_op | source)
XLA Modules:
  0.0 114.4 jit_solution(17048328096908181098)
XLA Ops:
  0.6 0.7 pad.14
  1.3 0.7 pad.15
  2.0 0.6 fusion.3.small_ref
  2.6 107.2 %shard_map.110 = (bf16[512,1280]{1,0:T(8,128)(2,1)}, bf16[56,16,640]{2,1,0:T(8,128)(2,1)}, f32[160,1920]{1,0:T(8,128)}, f32[1,240]{1,0:T(1,128)}, f32[1,160]{1,0:T(1,128)}) custom-call(s32[32]{0:T(128)} %dest_ref.1, s32[32]{0:T(128)} %amount_ref.1, f32[8,256]{1,0:T(8,128)} %fusion.3.small_ref, bf16[512,1280]{1,0:T(8,128)(2,1)} %x_hbm.1, ...), custom_call_target="tpu_custom_call" | custom-call | tf_op jit(solution)/shard_map/pallas_call | solution.py:563
  109.8 4.4 %shard_map.111 = (bf16[512,1280]{1,0:T(8,128)(2,1)}, bf16[56,16,640]{2,1,0:T(8,128)(2,1)}, f32[160,1920]{1,0:T(8,128)}, f32[1,240]{1,0:T(1,128)}, f32[1,160]{1,0:T(1,128)}) custom-call(bf16[512,1280]{1,0:T(8,128)(2,1)} %get-tuple-element.15.dx_in, bf16[56,16,640]{2,1,0:T(8,128)(2,1)} %get-tuple-element.16.att_in, f32[160,1920]{1,0:T(8,128)} %get-tuple-element.17.gw_in, ...), custom_call_target="tpu_custom_call" | custom-call | tf_op jit(solution)/shard_map/pallas_call | solution.py:647
  (2 shorter events, 0.0 us)

commit v4 on v3

--- a/solution.py
+++ b/solution.py
@@ -55,13 +55,17 @@
     return low, high - low
 
 
+def piece(h, i):
+    return pl.ds(SLOT * (i % 5), SLOT), pl.ds(*PUT[3 * h + i // 5])
+
+
 def block_kernel(
-    dest_ref, amount_ref, small_ref, x_hbm, w_hbm, grad_hbm,
-    dx_hbm, att_hbm, gw_hbm, gb_ref, gg_ref,
-    x_ref, grad_ref, dx_ref, out_ref, gw_ref,
-    wf, small_all, cmine, cbuf, stage, garr, tabs, csm, lane_sm, inverse_sm, slot_sm, starts,
+    dest_ref, amount_ref, bias_ref, gain_ref, x_hbm, w_hbm, grad_hbm,
+    dx_hbm, att_hbm, fin0, fin1, gb_ref, gg_ref,
+    x_ref, grad_ref, dx_ref, out_ref,
+    wf, small_ref, small_all, cmine, cbuf, stage, garr, tabs, csm, lane_sm, inverse_sm, slot_sm, starts,
     normed, normed_t, qkv, dqkv, g, att, probs, dn, inv, row, dgain, count_v, live_v,
-    lanes, arr, p_all, pair, ring_in, ring_out, tot, tot_small, plane0, plane1, fin0, fin1, sums, sums_all,
+    lanes, arr, p_all, pair, ring_in, ring_out, tot, tot_small, plane0, plane1, sums, sums_all,
     l_sem, c_sem, g_sem, s_sem, a_sem, z_sem, x_sem, y_sem, f_sem, w_send, w_recv, b_send, b_recv,
     p_send, p_recv, r_send, r_recv,
 ):
@@ -121,6 +125,8 @@
             have = jnp.where(lane // SLOT == i, amount_ref[8 * b + i], have)
         count_v[b : b + 1, :] = have
         live_v[b : b + 1, :] = jnp.where(lax.rem(lane, SLOT) < have, 1.0, 0.0)
+    small_ref[0:1, 0:240] = bias_ref[...].astype(F32).reshape(1, 240)
+    small_ref[1:2, 0:160] = gain_ref[...].astype(F32).reshape(1, 160)
     small_all[z] = small_ref[...]
     w_in.wait()
     pl.semaphore_wait(barrier, NDP - 1 + NZ - 1)
@@ -163,6 +169,7 @@
         return 0
 
     gather_start(0)
+    gather_start(1)
     lax.fori_loop(1, NDP, count_start, 0)
 
     for k in range(1, NZ):
@@ -198,8 +205,10 @@
 
     grad_in.wait()
     gather_step(0, 0)
+    gather_step(1, 0)
     lax.fori_loop(1, 16, grad_start, 0)
     gather_step(0, 1)
+    gather_step(1, 1)
     lax.fori_loop(16, NDP, grad_start, 0)
     garr[me, 0], garr[me, 1] = pick_grad(me)
 
@@ -271,23 +280,17 @@
             att[at] += o.astype(BF).reshape(8, SLOT, -1)
         return 0
 
-    def att_cols(h):
-        return pl.ds(256, 384) if h else pl.ds(0, 256)
-
-    def att_start(h, k, _):
+    def att_start(k, _):
         peer = lax.rem(me + k, NDP)
-        cols = att_cols(h)
         for i in range(2):
-            lanes[peer, i, :, cols] = att[inverse_sm[0, 0, 2 * peer + i], :, cols]
-        src, dst = lanes.at[peer, :, :, cols], arr.at[me, :, :, cols]
-        remote(src, dst, a_sem.at[h, 0], a_sem.at[h, 1], {"dp": peer}).start()
-        return 0
-
-    def att_send(h):
-        lax.fori_loop(1, NDP, functools.partial(att_start, h), 0)
-        cols = att_cols(h)
+            lanes[peer, i] = att[inverse_sm[0, 0, 2 * peer + i]]
+        remote(lanes.at[peer], arr.at[me], a_sem.at[0], a_sem.at[1], {"dp": peer}).start()
+        return 0
+
+    def att_send():
+        lax.fori_loop(1, NDP, att_start, 0)
         for i in range(2):
-            arr[me, i, :, cols] = att[inverse_sm[0, 0, 2 * me + i], :, cols]
+            arr[me, i] = att[inverse_sm[0, 0, 2 * me + i]]
 
     def take_grad(i, _):
         n = lane_sm[0, 0, i]
@@ -397,9 +400,6 @@
         for k in range(1, NZ):
             remote(sums, sums_all.at[z], z_sem.at[0], z_sem.at[1], {"fsdp": lax.rem(z + k, NZ)}).start()
 
-    def piece(h, i):
-        return pl.ds(SLOT * (i % 5), SLOT), pl.ds(*PUT[3 * h + i // 5])
-
     def scatter(h, i):
         src = tot_small.at[:, pl.ds(0, 384 if h else 256)] if i == PIECES - 1 else tot.at[piece(h, i)]
 
@@ -447,69 +447,54 @@
 
     out_scale = 1.0 / math.sqrt(NDP * NZ * ROWS)
 
-    def write_sums(h):
-        last_copy(h).wait()
-        for c in range(2):
-            for i in range(PIECES - 1):
-                rows, cols = piece(h, i)
-                gw_ref[pl.ds(rows.start + HALF * c, SLOT), cols] = fin[h][c, i].astype(F32) * out_scale
-
-    low_heads, high_heads = range(4), range(4, HEADS)
-    gather_step(0, 2)
-    gather_start(1)
-    gather_step(0, 3)
-    gather_end(0)
-    project(0)
-    gather_step(1, 0)
-    lax.fori_loop(0, 4, functools.partial(attend, low_heads), 0)
-    gather_step(1, 1)
-    att_send(0)
+    for s in range(2, 4):
+        for h in range(2):
+            gather_step(h, s)
+    for h in range(2):
+        gather_end(h)
+        project(h)
+    lax.fori_loop(0, 4, functools.partial(attend, range(HEADS)), 0)
     many(garr.at[pl.ds(0, NDP - 1)], g_sem).wait()
     lax.fori_loop(0, IMG, take_grad, 0)
-    lax.fori_loop(0, 4, functools.partial(attend_back, low_heads), 0)
-    gather_step(1, 2)
-    weight_grad(0, 4, 3, -3)
-    gather_step(1, 3)
+    lax.fori_loop(0, 4, functools.partial(attend_back, range(HEADS)), 0)
+    weight_grad(0, 4)
+    weight_grad(1, 4)
+    weight_grad(0, 3, -3)
     ring_step(0, 0)
-    weight_grad(0, 2, -2, 1, -1, 0)
-    gather_end(1)
-    project(1)
+    ring_step(1, 0)
+    att_send()
+    weight_grad(1, 3, -3)
+    weight_grad(0, 2, -2)
+    weight_grad(1, 2, -2)
     ring_step(0, 1)
-    lax.fori_loop(0, 4, functools.partial(attend, high_heads), 0)
-    ring_step(0, 2)
-    lax.fori_loop(0, 4, functools.partial(attend_back, high_heads), 0)
-    weight_grad(1, 4)
-    ring_step(0, 3)
-    weight_grad(1, 3, -3)
-    ring_step(1, 0)
-    att_send(1)
-    weight_grad(1, 2, -2)
+    weight_grad(0, 1, -1, 0)
     ring_step(1, 1)
     weight_grad(1, 1, -1, 0)
-    tot_small[...] = jnp.zeros_like(tot_small)
-    scatter(0, PIECES - 1)
-    ring_end(0)
-    for n in range(3):
-        input_grad(n)
+    input_grad(0)
+    input_grad(1)
+    ring_step(0, 2)
+    input_grad(2)
+    input_grad(3)
     ring_step(1, 2)
-    for n in range(3, 5):
-        input_grad(n)
+    input_grad(4)
     lax.fori_loop(0, 8, finish, 0)
-    ring_step(1, 3)
+    ring_step(0, 3)
     lax.fori_loop(8, 16, finish, 0)
     small_sums()
-    ring_end(1)
-    plane_sum(0)
+    ring_step(1, 3)
+    ring_end(0)
     many(sums_all.at[pl.ds(0, NZ - 1)], z_sem).wait()
     r = jnp.zeros((32, 128), F32)
     for s in range(NZ):
         r = r + sums_all[s].astype(F32)
     r = [jnp.concatenate([r[3 * i + j : 3 * i + j + 1, :] for j in range(3)], axis=1) for i in range(9)]
     tot_small[...] = jnp.concatenate(r + [jnp.zeros((7, 384), F32)], axis=0).astype(BF)
+    scatter(0, PIECES - 1)
     scatter(1, PIECES - 1)
-
-    for h in range(2):
-        many(arr.at[pl.ds(0, NDP - 1), :, :, att_cols(h)], a_sem.at[h]).wait()
+    ring_end(1)
+    plane_sum(0)
+
+    many(arr.at[pl.ds(0, NDP - 1)], a_sem).wait()
     slot_copy.wait()
 
     def place(i, _):
@@ -524,11 +509,9 @@
     lax.fori_loop(0, RECV, place, 0)
     att_out = pltpu.make_async_copy(out_ref, att_hbm, l_sem.at[1])
     att_out.start()
-    write_sums(0)
+    last_copy(0).wait()
     plane_end(1)
-    write_sums(1)
-    gw_out = pltpu.make_async_copy(gw_ref, gw_hbm, l_sem.at[2])
-    gw_out.start()
+    last_copy(1).wait()
     r = (fin1[0, PIECES - 1].astype(F32) + fin1[1, PIECES - 1].astype(F32)) * out_scale
     for i in range(25):
         part = r[i // 3 : i // 3 + 1, 128 * (i % 3) : 128 * (i % 3) + 128]
@@ -552,10 +535,9 @@
     remote(pair_like, pair_like, p_send, p_recv.at[0, 0], {"dp": sib}).wait_send()
     dx_out.wait()
     att_out.wait()
-    gw_out.wait()
-
-
-def block(dest, amount, small, x, weight, grad):
+
+
+def block(dest, amount, bias, gain, x, weight, grad):
     dma = pltpu.SemaphoreType.DMA
     vmem = pltpu.VMEM
     smem = pltpu.SMEM
@@ -565,19 +547,20 @@
         out_shape=(
             jax.ShapeDtypeStruct((ROWS, D), BF),
             jax.ShapeDtypeStruct((RECV, SLOT, W3), BF),
-            jax.ShapeDtypeStruct((SHARD, QKV), F32),
+            jax.ShapeDtypeStruct((2, CHIPS, SLOT, 256), BF),
+            jax.ShapeDtypeStruct((2, CHIPS, SLOT, 384), BF),
             jax.ShapeDtypeStruct((1, 240), F32),
             jax.ShapeDtypeStruct((1, 160), F32),
         ),
-        in_specs=[SM, SM, VM, ANY, ANY, ANY],
-        out_specs=(ANY, ANY, ANY, VM, VM),
+        in_specs=[SM, SM, VM, VM, ANY, ANY, ANY],
+        out_specs=(ANY, ANY, VM, VM, VM, VM),
         scratch_shapes=[
             vmem((ROWS, D), BF),
             vmem((RECV, SLOT, W3), BF),
             vmem((ROWS, D), BF),
             vmem((RECV, SLOT, W3), BF),
-            vmem((SHARD, QKV), F32),
             vmem((D, QKV), BF),
+            vmem((8, 256), F32),
             vmem((NZ, 8, 256), F32),
             vmem((1, 1, 128), i32),
             vmem((NDP, 1, 128), i32),
@@ -612,21 +595,21 @@
             vmem((SLOT, 384), BF),
             vmem((CHIPS, SLOT, 256), BF),
             vmem((CHIPS, SLOT, 384), BF),
-            vmem((2, CHIPS, SLOT, 256), BF),
-            vmem((2, CHIPS, SLOT, 384), BF),
             vmem((32, 128), BF),
             vmem((NZ, 32, 128), BF),
             dma((5,)),
-            dma((2,)), dma((2,)), dma((2,)), dma((2, 2)), dma((2,)), dma((2, 2)), dma((2, 2)), dma((2, 2)),
+            dma((2,)), dma((2,)), dma((2,)), dma((2,)), dma((2,)), dma((2, 2)), dma((2, 2)), dma((2, 2)),
             dma, dma((2, 4, 6)), dma, dma((2,)), dma, dma((2, 8)), dma, dma((2, 4, 6)),
         ],
         compiler_params=pltpu.CompilerParams(vmem_limit_bytes=LIMIT, collective_id=1, has_side_effects=True),
-    )(dest, amount, small, x, weight, grad)
-
-
-def hand_out_kernel(dx_in, att_in, gw_in, gb_in, gg_in, dx_out, att_out, gw_out, gb_out, gg_out, dx, att, gw, sems):
+    )(dest, amount, bias, gain, x, weight, grad)
+
+
+def hand_out_kernel(
+    dx_in, att_in, fin0, fin1, gb_in, gg_in, dx_out, att_out, gw_out, gb_out, gg_out, dx, att, sems
+):
     steps = []
-    for n, (src, mid, dst) in enumerate(((dx_in, dx, dx_out), (att_in, att, att_out), (gw_in, gw, gw_out))):
+    for n, (src, mid, dst) in enumerate(((dx_in, dx, dx_out), (att_in, att, att_out))):
         size = src.shape[0] // 4
         for i in range(4):
             part = pl.ds(size * i, size)
@@ -636,6 +619,12 @@
             steps.append((get, put))
     gb_out[...] = gb_in[...]
     gg_out[...] = gg_in[...]
+    out_scale = 1.0 / math.sqrt(NDP * NZ * ROWS)
+    for h, fin in enumerate((fin0, fin1)):
+        for c in range(2):
+            for i in range(PIECES - 1):
+                rows, cols = piece(h, i)
+                gw_out[pl.ds(rows.start + HALF * c, SLOT), cols] = fin[c, i].astype(F32) * out_scale
     for get, put in steps:
         get.wait()
         put.start()
@@ -643,24 +632,27 @@
         put.wait()
 
 
-def hand_out(*arrays):
+def hand_out(dx, att, fin0, fin1, gb, gg):
+    gw = jax.ShapeDtypeStruct((SHARD, QKV), F32)
     return pl.pallas_call(
         hand_out_kernel,
-        out_shape=tuple(jax.ShapeDtypeStruct(a.shape, a.dtype) for a in arrays),
-        in_specs=[ANY, ANY, ANY, VM, VM],
-        out_specs=(ANY, ANY, ANY, VM, VM),
-        scratch_shapes=[pltpu.VMEM(a.shape, a.dtype) for a in arrays[:3]] + [pltpu.SemaphoreType.DMA((2, 3, 4))],
+        out_shape=tuple(jax.ShapeDtypeStruct(a.shape, a.dtype) for a in (dx, att, gw, gb, gg)),
+        in_specs=[ANY, ANY, VM, VM, VM, VM],
+        out_specs=(ANY, ANY, VM, VM, VM),
+        scratch_shapes=[
+            pltpu.VMEM(dx.shape, dx.dtype),
+            pltpu.VMEM(att.shape, att.dtype),
+            pltpu.SemaphoreType.DMA((2, 2, 4)),
+        ],
         compiler_params=pltpu.CompilerParams(vmem_limit_bytes=LIMIT),
-    )(*arrays)
+    )(dx, att, fin0, fin1, gb, gg)
 
 
 def local(patches, patch_count, destination, qkv_weight, qkv_bias, norm_gain, grad_out):
-    small = jnp.stack([jnp.pad(qkv_bias, (0, 16)), jnp.pad(norm_gain, (0, 96))]).astype(F32)
-    small = jnp.pad(small, ((0, 6), (0, 0)))
-    dx, att, gw, gb, gg = block(
-        destination, patch_count, small, patches, qkv_weight, grad_out.reshape(RECV, SLOT, W3)
+    dx, att, fin0, fin1, gb, gg = block(
+        destination, patch_count, qkv_bias, norm_gain, patches, qkv_weight, grad_out.reshape(RECV, SLOT, W3)
     )
-    dx, att, gw, gb, gg = hand_out(dx, att, gw, gb, gg)
+    dx, att, gw, gb, gg = hand_out(dx, att, fin0, fin1, gb, gg)
     return att.reshape(RECV * SLOT, W3), dx, gw, gb.reshape(-1), gg.reshape(-1)
 
 

time: 115 us -> 107 us (0.930)
  Pallas kernels: 112 us -> 106 us
  local copies, waits for them, and re-layouts: 1.33 us -> 0 us
    pallas_call x1, Pallas kernels: 107 us -> 102 us  [block(): pl.pallas_call(block_kernel, out_shape=(jax.ShapeDtypeStruct((ROWS, D), B...]
    pad x2 -> x0, local copies, waits for them, and re-layouts: 1.32 us -> none  [the longest x1 0.66 us: local(): jnp.pad(qkv_bias, (0, 16))]
where the time goes in v4:
time: 107 us
  Pallas kernels  106 us (99%)
    pallas_call x1, Pallas kernels, block(): pl.pallas_call(block_kernel, out_shape=(jax.ShapeDtypeStruct((ROWS, D), B...  102 us
    pallas_call x1, Pallas kernels, hand_out(): pl.pallas_call(hand_out_kernel, out_shape=tuple((jax.ShapeDtypeStruct(a.s...  4.65 us

profile of v4, /device:TPU:1, one launch (start us, length us, event | category | flops | bytes accessed | tf_op | source)
XLA Modules:
  0.0 107.1 jit_solution(17985888135555393992)
XLA Ops:
  0.6 101.7 %shard_map.110 = (bf16[512,1280]{1,0:T(8,128)(2,1)}, bf16[56,16,640]{2,1,0:T(8,128)(2,1)}, bf16[2,16,16,256]{3,2,1,0:T(8,128)(2,1)}, bf16[2,16,16,384]{3,2,1,0:T...) custom-call(s32[32]{0:T(128)} %dest_ref.1, s32[32]{0:T(128)} %amount_ref.1, bf16[240]{0:T(256)(128)(2,1)} %bias_ref.1, ...), custom_call_target="tpu_custom_call" | custom-call | tf_op jit(solution)/shard_map/pallas_call | solution.py:545
  102.3 4.6 %shard_map.111 = (bf16[512,1280]{1,0:T(8,128)(2,1)}, bf16[56,16,640]{2,1,0:T(8,128)(2,1)}, f32[160,1920]{1,0:T(8,128)}, f32[1,240]{1,0:T(1,128)}, f32[1,160]{1,0:T(1,128)}) custom-call(bf16[512,1280]{1,0:T(8,128)(2,1)} %get-tuple-element.16.dx_in, bf16[56,16,640]{2,1,0:T(8,128)(2,1)} %get-tuple-element.17.att_in, ...), custom_call_target="tpu_custom_call" | custom-call | tf_op jit(solution)/shard_map/pallas_call | solution.py:637

commit v5 on v4

--- a/solution.py
+++ b/solution.py
@@ -275,7 +275,7 @@
             probs[b, h] = e / jnp.sum(e, axis=0, keepdims=True)
         for h in heads:
             v = own(h, qkv[rows, head_cols(h, 2)])
-            o = jnp.where(live, dot_nn(spread(probs[b, h]).T.astype(BF), v), 0.0)
+            o = jnp.where(live, dot_nn(spread(probs[b, h]).astype(BF).T, v), 0.0)
             at = pl.ds(pl.multiple_of(8 * b, 8), 8), slice(None), head_cols(h, 0)
             att[at] += o.astype(BF).reshape(8, SLOT, -1)
         return 0
@@ -307,9 +307,9 @@
             gh = jnp.where(live, own(h, gh), jnp.zeros((128, width), BF))
             p = probs[b, h]
             dp = compact(dot_nt(v, gh))
-            ds = spread(p * (dp - jnp.sum(dp * p, axis=0, keepdims=True)) * scale)
-            dq = dot_nn(ds.T.astype(BF), k)
-            dk = dot_nn(ds.astype(BF), q)
+            ds = spread(p * (dp - jnp.sum(dp * p, axis=0, keepdims=True)) * scale).astype(BF)
+            dq = dot_nn(ds.T, k)
+            dk = dot_nn(ds, q)
             dv = dot_nn(spread(p).astype(BF), gh)
             dqkv[rows, head_cols(h, 0)] += dq.astype(BF)
             dqkv[rows, head_cols(h, 1)] += dk.astype(BF)
@@ -470,17 +470,15 @@
     weight_grad(0, 1, -1, 0)
     ring_step(1, 1)
     weight_grad(1, 1, -1, 0)
-    input_grad(0)
-    input_grad(1)
+    for n in range(3):
+        input_grad(n)
     ring_step(0, 2)
-    input_grad(2)
     input_grad(3)
     ring_step(1, 2)
     input_grad(4)
-    lax.fori_loop(0, 8, finish, 0)
+    lax.fori_loop(0, 16, finish, 0)
+    small_sums()
     ring_step(0, 3)
-    lax.fori_loop(8, 16, finish, 0)
-    small_sums()
     ring_step(1, 3)
     ring_end(0)
     many(sums_all.at[pl.ds(0, NZ - 1)], z_sem).wait()
@@ -494,8 +492,6 @@
     ring_end(1)
     plane_sum(0)
 
-    many(arr.at[pl.ds(0, NDP - 1)], a_sem).wait()
-    slot_copy.wait()
 
     def place(i, _):
         n = slot_sm[0, 0, i]
@@ -506,6 +502,8 @@
 
     plane_sum(1)
     plane_end(0)
+    many(arr.at[pl.ds(0, NDP - 1)], a_sem).wait()
+    slot_copy.wait()
     lax.fori_loop(0, RECV, place, 0)
     att_out = pltpu.make_async_copy(out_ref, att_hbm, l_sem.at[1])
     att_out.start()

time: 107 us -> 107 us (level)
  no operation moved by 1% of the time
where the time goes in v5:
time: 107 us
  Pallas kernels  106 us (99%)
    pallas_call x1, Pallas kernels, block(): pl.pallas_call(block_kernel, out_shape=(jax.ShapeDtypeStruct((ROWS, D), B...  102 us
    pallas_call x1, Pallas kernels, hand_out(): pl.pallas_call(hand_out_kernel, out_shape=tuple((jax.ShapeDtypeStruct(a.s...  4.65 us

profile of v5, /device:TPU:1, one launch (start us, length us, event | category | flops | bytes accessed | tf_op | source)
XLA Modules:
  0.0 107.2 jit_solution(11512737727484085675)
XLA Ops:
  0.6 101.8 %shard_map.110 = (bf16[512,1280]{1,0:T(8,128)(2,1)}, bf16[56,16,640]{2,1,0:T(8,128)(2,1)}, bf16[2,16,16,256]{3,2,1,0:T(8,128)(2,1)}, bf16[2,16,16,384]{3,2,1,0:T...) custom-call(s32[32]{0:T(128)} %dest_ref.1, s32[32]{0:T(128)} %amount_ref.1, bf16[240]{0:T(256)(128)(2,1)} %bias_ref.1, ...), custom_call_target="tpu_custom_call" | custom-call | tf_op jit(solution)/shard_map/pallas_call | solution.py:543
  102.4 4.6 %shard_map.111 = (bf16[512,1280]{1,0:T(8,128)(2,1)}, bf16[56,16,640]{2,1,0:T(8,128)(2,1)}, f32[160,1920]{1,0:T(8,128)}, f32[1,240]{1,0:T(1,128)}, f32[1,160]{1,0:T(1,128)}) custom-call(bf16[512,1280]{1,0:T(8,128)(2,1)} %get-tuple-element.16.dx_in, bf16[56,16,640]{2,1,0:T(8,128)(2,1)} %get-tuple-element.17.att_in, ...), custom_call_target="tpu_custom_call" | custom-call | tf_op jit(solution)/shard_map/pallas_call | solution.py:635
